TPU v7x, 256 devices: a whole 4x4x8 slice. The times are simulated.
256 devices in a mesh: section: 16 (over z_hi, y), dp: 16 (over x, z_lo, core).
Axes of the slice: x: 4, y: 4, z: 8 (z_hi: 4, z_lo: 2; z = z_hi * 2 + z_lo), core: 2. Of those that a mesh axis runs over, the one named last changes fastest.
Arguments:
- acts: bfloat16 [16, 4, 512, 4096], P('section', None, 'dp'), may hold values from -6 to 6
- out_grad: bfloat16 [4, 512, 4096], P(None, 'dp'), may hold values from -6 to 6
- w_in: bfloat16 [16, 4096, 1152], P('section', 'dp'), may hold values from -0.09375 to 0.09375
- w_out: bfloat16 [16, 4096, 384], P('section', 'dp'), may hold values from -0.09375 to 0.09375
- decay_rate: float32 [16, 3], P('section'), may hold values from 0.004 to 0.04
- cycle_order: int32 [16], replicated, may hold values from 0 to 15, each once
Outputs:
- in_grad: bfloat16 [16, 4, 512, 4096], P('section', None, 'dp')
- grad_in: float32 [16, 4096, 1152], P('section', 'dp')
- grad_out: float32 [16, 4096, 384], P('section', 'dp')
Inputs may be any that keep to these rules, and one draw needn't show every extreme that they name: `cycle_order`: a permutation of the 16 replicas.
All inputs are finite; a program needn't handle non-finite values.
Results may differ from a plain program's by a relative error of at most 0.038.
Values may be sent and summed in bfloat16 or wider, within the bound.
A program may use at most 192 MiB of HBM per device.

v0:
```python
import jax
import jax.numpy as jnp
from jax import lax
from jax.sharding import PartitionSpec as P


def shifted(value, axis, steps):
    count = lax.axis_size(axis)
    initial, last = (max(0, -steps), min(count, count - steps))
    return lax.ppermute(value, axis, [(source, source + steps) for source in range(initial, last)])


def decay_table(rates, length):
    spots = jnp.arange(length).astype(jnp.float32)
    offset = spots[:, None] - spots[None, :]
    decayed = jnp.exp(-rates[:, None, None] * jnp.maximum(offset, 0.0)[None])
    return jnp.where(offset[None] >= 0.0, decayed, 0.0)


def contract_rows(left, right):
    return lax.dot_general(
        left, right, (((0,), (0,)), ((), ())), preferred_element_type=jnp.float32
    )


def contract_cols(left, right):
    return lax.dot_general(
        left, right, (((1,), (1,)), ((), ())), preferred_element_type=jnp.float32
    )


def retention_back(inputs, grad_y, weight_in, weight_out, table):
    length = inputs.shape[0]
    cols = weight_out.shape[1]
    heads = table.shape[0]
    head_size = cols // heads
    qkv = jnp.dot(inputs, weight_in, preferred_element_type=jnp.float32).astype(jnp.bfloat16)
    query = qkv[:, :cols].reshape(length, heads, head_size)
    keys = qkv[:, cols : 2 * cols].reshape(length, heads, head_size)
    values = qkv[:, 2 * cols :].reshape(length, heads, head_size)
    scores = (
        jnp.einsum("the,jhe->htj", query, keys, preferred_element_type=jnp.float32)
        * table
        / head_size
    ).astype(jnp.bfloat16)
    mixed = jnp.einsum("htj,jhe->the", scores, values, preferred_element_type=jnp.float32)
    mixed = mixed.reshape(length, cols).astype(jnp.bfloat16)
    d_mixed = jnp.dot(grad_y, weight_out, preferred_element_type=jnp.float32).astype(jnp.bfloat16)
    d_heads = d_mixed.reshape(length, heads, head_size)
    d_scores = (
        jnp.einsum("the,jhe->htj", d_heads, values, preferred_element_type=jnp.float32)
        * table
        / head_size
    ).astype(jnp.bfloat16)
    d_query = jnp.einsum("htj,jhe->the", d_scores, keys, preferred_element_type=jnp.float32)
    d_keys = jnp.einsum("htj,the->jhe", d_scores, query, preferred_element_type=jnp.float32)
    d_values = jnp.einsum("htj,the->jhe", scores, d_heads, preferred_element_type=jnp.float32)
    d_all = jnp.concatenate(
        [
            d_query.reshape(length, cols),
            d_keys.reshape(length, cols),
            d_values.reshape(length, cols),
        ],
        axis=1,
    ).astype(jnp.bfloat16)
    d_input = (grad_y.astype(jnp.float32) + contract_cols(d_all, weight_in)).astype(jnp.bfloat16)
    return (d_input, d_all, mixed)


def store(buffer, value, which, active):
    older = lax.dynamic_index_in_dim(buffer, which, 0, keepdims=False)
    return lax.dynamic_update_index_in_dim(buffer, jnp.where(active, value, older), which, 0)


def pass_back(d_input):
    return shifted(d_input, "section", -1)


def shards(acts, out_grad, w_in, w_out, decay_rate, cycle_order):
    sections = lax.axis_size("section")
    replicas = lax.axis_size("dp")
    place = lax.axis_index("section")
    replica = lax.axis_index("dp")
    full_in, full_out = (
        lax.all_gather(w_in[0], "dp", axis=0, tiled=True),
        lax.all_gather(w_out[0], "dp", axis=0, tiled=True),
    )
    micro = acts.shape[1]
    length = acts.shape[2]
    width = acts.shape[3]
    cols = full_out.shape[1]
    table = decay_table(decay_rate[0], length)
    saved = acts[0]
    live = jnp.where(replica == cycle_order[replicas - 1], 0.0, 1.0).astype(jnp.float32)
    last_section = sections - 1
    total_steps = micro + sections - 1

    def select(step):
        which = step - (last_section - place)
        active = jnp.logical_and(which >= 0, which < micro)
        return (jnp.clip(which, 0, micro - 1), active)

    def section_input(incoming, which):
        start_grad = lax.dynamic_index_in_dim(out_grad, which, 0, keepdims=False)
        return jnp.where(place == last_section, start_grad, incoming)

    def blank():
        return (
            jnp.zeros((length, width), jnp.bfloat16),
            jnp.zeros((length, 3 * cols), jnp.bfloat16),
            jnp.zeros((length, cols), jnp.bfloat16),
        )

    incoming0 = jnp.zeros((length, width), jnp.bfloat16)
    in_grads0 = jnp.zeros((micro, length, width), jnp.bfloat16)

    def advance(step, carry):
        incoming, in_grads, d_alls, mixes, grad_ys = carry
        which, active = select(step)
        grad_y = section_input(incoming, which)
        inputs = lax.dynamic_index_in_dim(saved, which, 0, keepdims=False)
        d_input, d_all, mixed = lax.cond(
            active, lambda: retention_back(inputs, grad_y, full_in, full_out, table), blank
        )
        in_grads = store(in_grads, d_input, which, active)
        d_alls = store(d_alls, d_all, which, active)
        mixes = store(mixes, mixed, which, active)
        grad_ys = store(grad_ys, grad_y, which, active)
        incoming = pass_back(d_input)
        return (incoming, in_grads, d_alls, mixes, grad_ys)

    start = (
        incoming0,
        in_grads0,
        jnp.zeros((micro, length, 3 * cols), jnp.bfloat16),
        jnp.zeros((micro, length, cols), jnp.bfloat16),
        jnp.zeros((micro, length, width), jnp.bfloat16),
    )
    _, in_grads, d_alls, mixes, grad_ys = lax.fori_loop(0, total_steps, advance, start)
    flat_inputs = saved.reshape(micro * length, width)
    flat_grads = grad_ys.reshape(micro * length, width)
    flat_dall = d_alls.reshape(micro * length, 3 * cols)
    flat_mixed = mixes.reshape(micro * length, cols)
    left_part = contract_rows(flat_inputs, flat_dall)
    right_part = contract_rows(flat_grads, flat_mixed)
    summed = lax.psum_scatter(
        (jnp.concatenate([left_part, right_part], axis=1) * live).astype(jnp.bfloat16),
        "dp",
        scatter_dimension=0,
        tiled=True,
    ).astype(jnp.float32)
    scale = 1.0 / (replicas - 1.0)
    grad_in = (summed[:, : 3 * cols] * scale)[None]
    grad_out = (summed[:, 3 * cols :] * scale)[None]
    return (in_grads[None], grad_in, grad_out)


def solution(mesh):
    placed = (
        P("section", None, "dp", None),
        P(None, "dp", None),
        P("section", "dp", None),
        P("section", "dp", None),
        P("section", None),
        P(),
    )
    return jax.shard_map(
        shards,
        mesh=mesh,
        in_specs=placed,
        out_specs=(
            P("section", None, "dp", None),
            P("section", "dp", None),
            P("section", "dp", None),
        ),
        check_vma=False,
    )
```

profile of v0, /device:TPU:33, one launch (start us, length us, event | category | flops | bytes accessed | tf_op | source)
XLA Modules:
  0.0 763.0 jit_solution(17528883123188055466)
XLA Ops:
  11.4 39.4 %all-gather.7.cloned.1.call-done = bf16[1,4096,384]{2,1,0:T(8,128)(2,1)} async-done(((bf16[1,256,384]{2,1,0:T(8,128)(2,1)}), bf16[1,4096,384]{2,1,0:T(8,128)(2,1)}) %all-gather.7.cloned.1.call-update) | async-done | bytes 3145744 | tf_op jit(solution)/shard_map/all_gather | solution.py:86
  50.9 62.0 %all-gather.5.cloned.1.call-done = bf16[1,4096,1152]{2,1,0:T(8,128)(2,1)} async-done(((bf16[1,256,1152]{2,1,0:T(8,128)(2,1)}), bf16[1,4096,1152]{2,1,0:T(8,128)(2,1)}) %all-gather.5.cloned.1.call-update) | async-done | bytes 9437200 | tf_op jit(solution)/shard_map/all_gather | solution.py:85
  113.1 478.7 %while.24 = (s32[]{:T(128)}, bf16[32,4096]{1,0:T(8,128)(2,1)S(1)}, bf16[4,32,4096]{2,1,0:T(8,128)(2,1)S(1)}, bf16[4,32,1152]{2,1,0:T(8,128)(2,1)S(1)}, bf16[4,32...) while((s32[]{:T(128)}, bf16[32,4096]{1,0:T(8,128)(2,1)S(1)}, ...), condition=%wide.region_3.4_spmd.clone, body=%wide.region_0.3_spmd.clone.sunk | while | flops 710326272 | bytes 56925164 | solution.py:139
  116.5 8.0 %collective-permute-done = bf16[32,4096]{1,0:T(8,128)(2,1)S(1)} collective-permute-done((bf16[32,4096]{1,0:T(8,128)(2,1)S(1)}, bf16[32,4096]{1,0:T(8,128)(2,1)S(1)}, u32[]{:S(2)}, u32[]{:S(2)}) %collective-permute-start) | collective-permute-done | bytes 262176 | tf_op jit(solution)/shard_map/while/body/eval_jaxpr/ppermute | solution.py:10
  127.8 7.1 collective-permute-done
  138.2 6.2 collective-permute-done
  147.7 10.3 %collective-permute-done = bf16[32,4096]{1,0:T(8,128)(2,1)S(1)} collective-permute-done((bf16[32,4096]{1,0:T(8,128)(2,1)S(1)}, bf16[32,4096]{1,0:T(8,128)(2,1)S(1)}, u32[]{:S(2)}, u32[]{:S(2)}) %collective-permute-start) | collective-permute-done | bytes 262176 | tf_op jit(solution)/shard_map/while/body/eval_jaxpr/ppermute | solution.py:10
  161.3 7.3 collective-permute-done
  171.9 11.9 %collective-permute-done = bf16[32,4096]{1,0:T(8,128)(2,1)S(1)} collective-permute-done((bf16[32,4096]{1,0:T(8,128)(2,1)S(1)}, bf16[32,4096]{1,0:T(8,128)(2,1)S(1)}, u32[]{:S(2)}, u32[]{:S(2)}) %collective-permute-start) | collective-permute-done | bytes 262176 | tf_op jit(solution)/shard_map/while/body/eval_jaxpr/ppermute | solution.py:10
  187.1 9.6 %collective-permute-done = bf16[32,4096]{1,0:T(8,128)(2,1)S(1)} collective-permute-done((bf16[32,4096]{1,0:T(8,128)(2,1)S(1)}, bf16[32,4096]{1,0:T(8,128)(2,1)S(1)}, u32[]{:S(2)}, u32[]{:S(2)}) %collective-permute-start) | collective-permute-done | bytes 262176 | tf_op jit(solution)/shard_map/while/body/eval_jaxpr/ppermute | solution.py:10
  200.0 8.1 %collective-permute-done = bf16[32,4096]{1,0:T(8,128)(2,1)S(1)} collective-permute-done((bf16[32,4096]{1,0:T(8,128)(2,1)S(1)}, bf16[32,4096]{1,0:T(8,128)(2,1)S(1)}, u32[]{:S(2)}, u32[]{:S(2)}) %collective-permute-start) | collective-permute-done | bytes 262176 | tf_op jit(solution)/shard_map/while/body/eval_jaxpr/ppermute | solution.py:10
  211.4 9.0 %collective-permute-done = bf16[32,4096]{1,0:T(8,128)(2,1)S(1)} collective-permute-done((bf16[32,4096]{1,0:T(8,128)(2,1)S(1)}, bf16[32,4096]{1,0:T(8,128)(2,1)S(1)}, u32[]{:S(2)}, u32[]{:S(2)}) %collective-permute-start) | collective-permute-done | bytes 262176 | tf_op jit(solution)/shard_map/while/body/eval_jaxpr/ppermute | solution.py:10
  223.7 18.4 %collective-permute-done = bf16[32,4096]{1,0:T(8,128)(2,1)S(1)} collective-permute-done((bf16[32,4096]{1,0:T(8,128)(2,1)S(1)}, bf16[32,4096]{1,0:T(8,128)(2,1)S(1)}, u32[]{:S(2)}, u32[]{:S(2)}) %collective-permute-start) | collective-permute-done | bytes 262176 | tf_op jit(solution)/shard_map/while/body/eval_jaxpr/ppermute | solution.py:10
  245.4 12.3 %collective-permute-done = bf16[32,4096]{1,0:T(8,128)(2,1)S(1)} collective-permute-done((bf16[32,4096]{1,0:T(8,128)(2,1)S(1)}, bf16[32,4096]{1,0:T(8,128)(2,1)S(1)}, u32[]{:S(2)}, u32[]{:S(2)}) %collective-permute-start) | collective-permute-done | bytes 262176 | tf_op jit(solution)/shard_map/while/body/eval_jaxpr/ppermute | solution.py:10
  260.9 18.0 %collective-permute-done = bf16[32,4096]{1,0:T(8,128)(2,1)S(1)} collective-permute-done((bf16[32,4096]{1,0:T(8,128)(2,1)S(1)}, bf16[32,4096]{1,0:T(8,128)(2,1)S(1)}, u32[]{:S(2)}, u32[]{:S(2)}) %collective-permute-start) | collective-permute-done | bytes 262176 | tf_op jit(solution)/shard_map/while/body/eval_jaxpr/ppermute | solution.py:10
  282.2 5.6 collective-permute-done
  291.2 6.2 collective-permute-done
  300.7 164.9 %collective-permute-done = bf16[32,4096]{1,0:T(8,128)(2,1)S(1)} collective-permute-done((bf16[32,4096]{1,0:T(8,128)(2,1)S(1)}, bf16[32,4096]{1,0:T(8,128)(2,1)S(1)}, u32[]{:S(2)}, u32[]{:S(2)}) %collective-permute-start) | collective-permute-done | bytes 262176 | tf_op jit(solution)/shard_map/while/body/eval_jaxpr/ppermute | solution.py:10
  466.7 14.7 %conditional.3 = (bf16[32,4096]{1,0:T(8,128)(2,1)S(1)}, bf16[32,1152]{1,0:T(8,128)(2,1)}, bf16[32,384]{1,0:T(8,128)(2,1)S(1)}) conditional(s32[]{:T(128)} %convert_element_type.90, () %tuple.68, (bf16[32,4096]{1,0:T(8,128)(2,1)S(1)}, bf16[4,32,4096]{2,1,0:T(8,128)(2,1)}, s32[]{:T(128)}, bf16[4096,1152]{1,0:T(8,128)(2,1)}, ...), branch_computations={%region_1.1_spmd, %region_2.2_spmd.clone} | conditional | flops 709883904 | bytes 52238968 | solution.py:122
  469.3 5.5 convolution_convert_fusion
  483.8 9.9 %collective-permute-done = bf16[32,4096]{1,0:T(8,128)(2,1)S(1)} collective-permute-done((bf16[32,4096]{1,0:T(8,128)(2,1)S(1)}, bf16[32,4096]{1,0:T(8,128)(2,1)S(1)}, u32[]{:S(2)}, u32[]{:S(2)}) %collective-permute-start) | collective-permute-done | bytes 262176 | tf_op jit(solution)/shard_map/while/body/eval_jaxpr/ppermute | solution.py:10
  494.9 14.7 %conditional.3 = (bf16[32,4096]{1,0:T(8,128)(2,1)S(1)}, bf16[32,1152]{1,0:T(8,128)(2,1)}, bf16[32,384]{1,0:T(8,128)(2,1)S(1)}) conditional(s32[]{:T(128)} %convert_element_type.90, () %tuple.68, (bf16[32,4096]{1,0:T(8,128)(2,1)S(1)}, bf16[4,32,4096]{2,1,0:T(8,128)(2,1)}, s32[]{:T(128)}, bf16[4096,1152]{1,0:T(8,128)(2,1)}, ...), branch_computations={%region_1.1_spmd, %region_2.2_spmd.clone} | conditional | flops 709883904 | bytes 52238968 | solution.py:122
  497.5 5.5 convolution_convert_fusion
  512.0 22.7 %collective-permute-done = bf16[32,4096]{1,0:T(8,128)(2,1)S(1)} collective-permute-done((bf16[32,4096]{1,0:T(8,128)(2,1)S(1)}, bf16[32,4096]{1,0:T(8,128)(2,1)S(1)}, u32[]{:S(2)}, u32[]{:S(2)}) %collective-permute-start) | collective-permute-done | bytes 262176 | tf_op jit(solution)/shard_map/while/body/eval_jaxpr/ppermute | solution.py:10
  535.8 14.7 %conditional.3 = (bf16[32,4096]{1,0:T(8,128)(2,1)S(1)}, bf16[32,1152]{1,0:T(8,128)(2,1)}, bf16[32,384]{1,0:T(8,128)(2,1)S(1)}) conditional(s32[]{:T(128)} %convert_element_type.90, () %tuple.68, (bf16[32,4096]{1,0:T(8,128)(2,1)S(1)}, bf16[4,32,4096]{2,1,0:T(8,128)(2,1)}, s32[]{:T(128)}, bf16[4096,1152]{1,0:T(8,128)(2,1)}, ...), branch_computations={%region_1.1_spmd, %region_2.2_spmd.clone} | conditional | flops 709883904 | bytes 52238968 | solution.py:122
  538.5 5.5 convolution_convert_fusion
  553.0 15.9 %collective-permute-done = bf16[32,4096]{1,0:T(8,128)(2,1)S(1)} collective-permute-done((bf16[32,4096]{1,0:T(8,128)(2,1)S(1)}, bf16[32,4096]{1,0:T(8,128)(2,1)S(1)}, u32[]{:S(2)}, u32[]{:S(2)}) %collective-permute-start) | collective-permute-done | bytes 262176 | tf_op jit(solution)/shard_map/while/body/eval_jaxpr/ppermute | solution.py:10
  569.9 14.7 %conditional.3 = (bf16[32,4096]{1,0:T(8,128)(2,1)S(1)}, bf16[32,1152]{1,0:T(8,128)(2,1)}, bf16[32,384]{1,0:T(8,128)(2,1)S(1)}) conditional(s32[]{:T(128)} %convert_element_type.90, () %tuple.68, (bf16[32,4096]{1,0:T(8,128)(2,1)S(1)}, bf16[4,32,4096]{2,1,0:T(8,128)(2,1)}, s32[]{:T(128)}, bf16[4096,1152]{1,0:T(8,128)(2,1)}, ...), branch_computations={%region_1.1_spmd, %region_2.2_spmd.clone} | conditional | flops 709883904 | bytes 52238968 | solution.py:122
  572.6 5.5 convolution_convert_fusion
  587.1 4.7 collective-permute-done
  596.7 9.0 %fusion.32 = bf16[4096,1536]{0,1:T(8,128)(2,1)} fusion(f32[4096,384]{0,1:T(8,128)S(1)} %convolution_bitcast_fusion.1, f32[4096,1152]{0,1:T(8,128)S(1)} %convolution_bitcast_fusion, f32[]{:T(128)S(6)} %select_n.115), kind=kLoop, calls=%fused_computation.62 | loop fusion | flops 18874368 | bytes 37748740 | tf_op jit(solution)/shard_map/convert_element_type | solution.py:147
  605.8 147.0 %reduce-scatter.2.cloned.1.call-done = bf16[256,1536]{0,1:T(8,128)(2,1)} async-done(((bf16[4096,1536]{0,1:T(8,128)(2,1)}), bf16[256,1536]{0,1:T(8,128)(2,1)}) %reduce-scatter.2.cloned.1.call-update) | async-done | bytes 786448 | tf_op jit(solution)/shard_map/reduce_scatter | solution.py:146
  (336 shorter events, 121.4 us)
Async XLA Ops:
  7.2 43.7 %all-gather.7.cloned.1.call-start = ((), (), s32[]{:S(2)}) async-start(), calls=%async_computation.3 | async-start | bytes 3342336 | tf_op jit(solution)/shard_map/all_gather | solution.py:86
  7.9 104.9 %all-gather.5.cloned.1.call-start = ((), (), s32[]{:S(2)}) async-start(), calls=%async_computation.2 | async-start | bytes 10027008 | tf_op jit(solution)/shard_map/all_gather | solution.py:85
  8.6 744.1 %reduce-scatter.2.cloned.1.call-start = ((), (), s32[]{:S(2)}) async-start(), calls=%async_computation.1 | async-start | bytes 13369344 | tf_op jit(solution)/shard_map/reduce_scatter | solution.py:146
  114.9 9.5 %collective-permute-start = (bf16[32,4096]{1,0:T(8,128)(2,1)S(1)}, bf16[32,4096]{1,0:T(8,128)(2,1)S(1)}, u32[]{:S(2)}, u32[]{:S(2)}) collective-permute-start(bf16[32,4096]{1,0:T(8,128)(2,1)S(1)} %get-tuple-element.528), channel_id=1, source_target_pairs={{16,0},{32,16},{48,32},{64,48},{80,64},{96,80},{112,96},{128,112},... | collective-permute-start | bytes 786440 | tf_op jit(solution)/shard_map/while/body/eval_jaxpr/ppermute | solution.py:10
  126.3 8.6 %collective-permute-start = (bf16[32,4096]{1,0:T(8,128)(2,1)S(1)}, bf16[32,4096]{1,0:T(8,128)(2,1)S(1)}, u32[]{:S(2)}, u32[]{:S(2)}) collective-permute-start(bf16[32,4096]{1,0:T(8,128)(2,1)S(1)} %get-tuple-element.528), channel_id=1, source_target_pairs={{16,0},{32,16},{48,32},{64,48},{80,64},{96,80},{112,96},{128,112},... | collective-permute-start | bytes 786440 | tf_op jit(solution)/shard_map/while/body/eval_jaxpr/ppermute | solution.py:10
  136.7 7.7 %collective-permute-start = (bf16[32,4096]{1,0:T(8,128)(2,1)S(1)}, bf16[32,4096]{1,0:T(8,128)(2,1)S(1)}, u32[]{:S(2)}, u32[]{:S(2)}) collective-permute-start(bf16[32,4096]{1,0:T(8,128)(2,1)S(1)} %get-tuple-element.528), channel_id=1, source_target_pairs={{16,0},{32,16},{48,32},{64,48},{80,64},{96,80},{112,96},{128,112},... | collective-permute-start | bytes 786440 | tf_op jit(solution)/shard_map/while/body/eval_jaxpr/ppermute | solution.py:10
  146.2 11.8 %collective-permute-start = (bf16[32,4096]{1,0:T(8,128)(2,1)S(1)}, bf16[32,4096]{1,0:T(8,128)(2,1)S(1)}, u32[]{:S(2)}, u32[]{:S(2)}) collective-permute-start(bf16[32,4096]{1,0:T(8,128)(2,1)S(1)} %get-tuple-element.528), channel_id=1, source_target_pairs={{16,0},{32,16},{48,32},{64,48},{80,64},{96,80},{112,96},{128,112},... | collective-permute-start | bytes 786440 | tf_op jit(solution)/shard_map/while/body/eval_jaxpr/ppermute | solution.py:10
  159.8 8.9 %collective-permute-start = (bf16[32,4096]{1,0:T(8,128)(2,1)S(1)}, bf16[32,4096]{1,0:T(8,128)(2,1)S(1)}, u32[]{:S(2)}, u32[]{:S(2)}) collective-permute-start(bf16[32,4096]{1,0:T(8,128)(2,1)S(1)} %get-tuple-element.528), channel_id=1, source_target_pairs={{16,0},{32,16},{48,32},{64,48},{80,64},{96,80},{112,96},{128,112},... | collective-permute-start | bytes 786440 | tf_op jit(solution)/shard_map/while/body/eval_jaxpr/ppermute | solution.py:10
  170.4 13.4 %collective-permute-start = (bf16[32,4096]{1,0:T(8,128)(2,1)S(1)}, bf16[32,4096]{1,0:T(8,128)(2,1)S(1)}, u32[]{:S(2)}, u32[]{:S(2)}) collective-permute-start(bf16[32,4096]{1,0:T(8,128)(2,1)S(1)} %get-tuple-element.528), channel_id=1, source_target_pairs={{16,0},{32,16},{48,32},{64,48},{80,64},{96,80},{112,96},{128,112},... | collective-permute-start | bytes 786440 | tf_op jit(solution)/shard_map/while/body/eval_jaxpr/ppermute | solution.py:10
  185.6 11.1 %collective-permute-start = (bf16[32,4096]{1,0:T(8,128)(2,1)S(1)}, bf16[32,4096]{1,0:T(8,128)(2,1)S(1)}, u32[]{:S(2)}, u32[]{:S(2)}) collective-permute-start(bf16[32,4096]{1,0:T(8,128)(2,1)S(1)} %get-tuple-element.528), channel_id=1, source_target_pairs={{16,0},{32,16},{48,32},{64,48},{80,64},{96,80},{112,96},{128,112},... | collective-permute-start | bytes 786440 | tf_op jit(solution)/shard_map/while/body/eval_jaxpr/ppermute | solution.py:10
  198.5 9.6 %collective-permute-start = (bf16[32,4096]{1,0:T(8,128)(2,1)S(1)}, bf16[32,4096]{1,0:T(8,128)(2,1)S(1)}, u32[]{:S(2)}, u32[]{:S(2)}) collective-permute-start(bf16[32,4096]{1,0:T(8,128)(2,1)S(1)} %get-tuple-element.528), channel_id=1, source_target_pairs={{16,0},{32,16},{48,32},{64,48},{80,64},{96,80},{112,96},{128,112},... | collective-permute-start | bytes 786440 | tf_op jit(solution)/shard_map/while/body/eval_jaxpr/ppermute | solution.py:10
  209.9 10.5 %collective-permute-start = (bf16[32,4096]{1,0:T(8,128)(2,1)S(1)}, bf16[32,4096]{1,0:T(8,128)(2,1)S(1)}, u32[]{:S(2)}, u32[]{:S(2)}) collective-permute-start(bf16[32,4096]{1,0:T(8,128)(2,1)S(1)} %get-tuple-element.528), channel_id=1, source_target_pairs={{16,0},{32,16},{48,32},{64,48},{80,64},{96,80},{112,96},{128,112},... | collective-permute-start | bytes 786440 | tf_op jit(solution)/shard_map/while/body/eval_jaxpr/ppermute | solution.py:10
  222.2 19.9 %collective-permute-start = (bf16[32,4096]{1,0:T(8,128)(2,1)S(1)}, bf16[32,4096]{1,0:T(8,128)(2,1)S(1)}, u32[]{:S(2)}, u32[]{:S(2)}) collective-permute-start(bf16[32,4096]{1,0:T(8,128)(2,1)S(1)} %get-tuple-element.528), channel_id=1, source_target_pairs={{16,0},{32,16},{48,32},{64,48},{80,64},{96,80},{112,96},{128,112},... | collective-permute-start | bytes 786440 | tf_op jit(solution)/shard_map/while/body/eval_jaxpr/ppermute | solution.py:10
  243.8 13.8 %collective-permute-start = (bf16[32,4096]{1,0:T(8,128)(2,1)S(1)}, bf16[32,4096]{1,0:T(8,128)(2,1)S(1)}, u32[]{:S(2)}, u32[]{:S(2)}) collective-permute-start(bf16[32,4096]{1,0:T(8,128)(2,1)S(1)} %get-tuple-element.528), channel_id=1, source_target_pairs={{16,0},{32,16},{48,32},{64,48},{80,64},{96,80},{112,96},{128,112},... | collective-permute-start | bytes 786440 | tf_op jit(solution)/shard_map/while/body/eval_jaxpr/ppermute | solution.py:10
  259.4 19.5 %collective-permute-start = (bf16[32,4096]{1,0:T(8,128)(2,1)S(1)}, bf16[32,4096]{1,0:T(8,128)(2,1)S(1)}, u32[]{:S(2)}, u32[]{:S(2)}) collective-permute-start(bf16[32,4096]{1,0:T(8,128)(2,1)S(1)} %get-tuple-element.528), channel_id=1, source_target_pairs={{16,0},{32,16},{48,32},{64,48},{80,64},{96,80},{112,96},{128,112},... | collective-permute-start | bytes 786440 | tf_op jit(solution)/shard_map/while/body/eval_jaxpr/ppermute | solution.py:10
  280.7 7.1 collective-permute-start
  289.6 7.8 %collective-permute-start = (bf16[32,4096]{1,0:T(8,128)(2,1)S(1)}, bf16[32,4096]{1,0:T(8,128)(2,1)S(1)}, u32[]{:S(2)}, u32[]{:S(2)}) collective-permute-start(bf16[32,4096]{1,0:T(8,128)(2,1)S(1)} %get-tuple-element.528), channel_id=1, source_target_pairs={{16,0},{32,16},{48,32},{64,48},{80,64},{96,80},{112,96},{128,112},... | collective-permute-start | bytes 786440 | tf_op jit(solution)/shard_map/while/body/eval_jaxpr/ppermute | solution.py:10
  299.2 166.4 %collective-permute-start = (bf16[32,4096]{1,0:T(8,128)(2,1)S(1)}, bf16[32,4096]{1,0:T(8,128)(2,1)S(1)}, u32[]{:S(2)}, u32[]{:S(2)}) collective-permute-start(bf16[32,4096]{1,0:T(8,128)(2,1)S(1)} %get-tuple-element.528), channel_id=1, source_target_pairs={{16,0},{32,16},{48,32},{64,48},{80,64},{96,80},{112,96},{128,112},... | collective-permute-start | bytes 786440 | tf_op jit(solution)/shard_map/while/body/eval_jaxpr/ppermute | solution.py:10
  466.7 10.9 %slice-start = ((s8[9437184]{0:T(1024)(128)(4,1)}), s8[4194304]{0:T(1024)(128)(4,1)S(1)}, s32[]{:S(2)}) async-start(s8[9437184]{0:T(1024)(128)(4,1)} %bitcast.131), calls=%async_computation.4 | async-start | bytes 8388608 | tf_op jit(solution)/shard_map/while/body/eval_jaxpr/cond
  469.3 8.3 %slice-start.1 = ((s8[9437184]{0:T(1024)(128)(4,1)}), s8[4194304]{0:T(1024)(128)(4,1)S(1)}, s32[]{:S(2)}) async-start(s8[9437184]{0:T(1024)(128)(4,1)} %bitcast.131), calls=%async_computation.5 | async-start | bytes 8388608 | tf_op jit(solution)/shard_map/while/body/eval_jaxpr/cond
  469.3 8.3 %slice-start.2 = ((s8[9437184]{0:T(1024)(128)(4,1)}), s8[1048576]{0:T(1024)(128)(4,1)S(1)}, s32[]{:S(2)}) async-start(s8[9437184]{0:T(1024)(128)(4,1)} %bitcast.131), calls=%async_computation.6 | async-start | bytes 2097152 | tf_op jit(solution)/shard_map/while/body/eval_jaxpr/cond
  481.4 12.3 %collective-permute-start = (bf16[32,4096]{1,0:T(8,128)(2,1)S(1)}, bf16[32,4096]{1,0:T(8,128)(2,1)S(1)}, u32[]{:S(2)}, u32[]{:S(2)}) collective-permute-start(bf16[32,4096]{1,0:T(8,128)(2,1)S(1)} %get-tuple-element.528), channel_id=1, source_target_pairs={{16,0},{32,16},{48,32},{64,48},{80,64},{96,80},{112,96},{128,112},... | collective-permute-start | bytes 786440 | tf_op jit(solution)/shard_map/while/body/eval_jaxpr/ppermute | solution.py:10
  494.9 10.9 %slice-start = ((s8[9437184]{0:T(1024)(128)(4,1)}), s8[4194304]{0:T(1024)(128)(4,1)S(1)}, s32[]{:S(2)}) async-start(s8[9437184]{0:T(1024)(128)(4,1)} %bitcast.131), calls=%async_computation.4 | async-start | bytes 8388608 | tf_op jit(solution)/shard_map/while/body/eval_jaxpr/cond
  497.5 8.3 %slice-start.1 = ((s8[9437184]{0:T(1024)(128)(4,1)}), s8[4194304]{0:T(1024)(128)(4,1)S(1)}, s32[]{:S(2)}) async-start(s8[9437184]{0:T(1024)(128)(4,1)} %bitcast.131), calls=%async_computation.5 | async-start | bytes 8388608 | tf_op jit(solution)/shard_map/while/body/eval_jaxpr/cond
  509.6 25.1 %collective-permute-start = (bf16[32,4096]{1,0:T(8,128)(2,1)S(1)}, bf16[32,4096]{1,0:T(8,128)(2,1)S(1)}, u32[]{:S(2)}, u32[]{:S(2)}) collective-permute-start(bf16[32,4096]{1,0:T(8,128)(2,1)S(1)} %get-tuple-element.528), channel_id=1, source_target_pairs={{16,0},{32,16},{48,32},{64,48},{80,64},{96,80},{112,96},{128,112},... | collective-permute-start | bytes 786440 | tf_op jit(solution)/shard_map/while/body/eval_jaxpr/ppermute | solution.py:10
  535.9 10.9 %slice-start = ((s8[9437184]{0:T(1024)(128)(4,1)}), s8[4194304]{0:T(1024)(128)(4,1)S(1)}, s32[]{:S(2)}) async-start(s8[9437184]{0:T(1024)(128)(4,1)} %bitcast.131), calls=%async_computation.4 | async-start | bytes 8388608 | tf_op jit(solution)/shard_map/while/body/eval_jaxpr/cond
  538.5 8.3 %slice-start.1 = ((s8[9437184]{0:T(1024)(128)(4,1)}), s8[4194304]{0:T(1024)(128)(4,1)S(1)}, s32[]{:S(2)}) async-start(s8[9437184]{0:T(1024)(128)(4,1)} %bitcast.131), calls=%async_computation.5 | async-start | bytes 8388608 | tf_op jit(solution)/shard_map/while/body/eval_jaxpr/cond
  550.6 18.3 %collective-permute-start = (bf16[32,4096]{1,0:T(8,128)(2,1)S(1)}, bf16[32,4096]{1,0:T(8,128)(2,1)S(1)}, u32[]{:S(2)}, u32[]{:S(2)}) collective-permute-start(bf16[32,4096]{1,0:T(8,128)(2,1)S(1)} %get-tuple-element.528), channel_id=1, source_target_pairs={{16,0},{32,16},{48,32},{64,48},{80,64},{96,80},{112,96},{128,112},... | collective-permute-start | bytes 786440 | tf_op jit(solution)/shard_map/while/body/eval_jaxpr/ppermute | solution.py:10
  570.0 10.9 %slice-start = ((s8[9437184]{0:T(1024)(128)(4,1)}), s8[4194304]{0:T(1024)(128)(4,1)S(1)}, s32[]{:S(2)}) async-start(s8[9437184]{0:T(1024)(128)(4,1)} %bitcast.131), calls=%async_computation.4 | async-start | bytes 8388608 | tf_op jit(solution)/shard_map/while/body/eval_jaxpr/cond
  572.6 8.3 %slice-start.1 = ((s8[9437184]{0:T(1024)(128)(4,1)}), s8[4194304]{0:T(1024)(128)(4,1)S(1)}, s32[]{:S(2)}) async-start(s8[9437184]{0:T(1024)(128)(4,1)} %bitcast.131), calls=%async_computation.5 | async-start | bytes 8388608 | tf_op jit(solution)/shard_map/while/body/eval_jaxpr/cond
  572.6 8.3 %slice-start.2 = ((s8[9437184]{0:T(1024)(128)(4,1)}), s8[1048576]{0:T(1024)(128)(4,1)S(1)}, s32[]{:S(2)}) async-start(s8[9437184]{0:T(1024)(128)(4,1)} %bitcast.131), calls=%async_computation.6 | async-start | bytes 2097152 | tf_op jit(solution)/shard_map/while/body/eval_jaxpr/cond
  584.7 7.1 collective-permute-start
  (3 other events, 21.6 us)
Sparse Core Ops, SparseCore 0:
  9.8 40.9 all-gather.6
  52.7 60.0 all-gather.4
  605.9 146.7 reduce-scatter.1
where the time goes:
time: 767 us; the launch traced here: 763 us
  waiting for transfers between devices  606 us (79%)
  matrix products  55.9 us (7%)
  other arithmetic  37.4 us (5%)
  starting transfers between devices  24.7 us (3%)
  local copies, waits for them, and re-layouts  22.7 us (3%)
  between operations  14.5 us (2%)
    ppermute x19, waiting for transfers between devices, shifted(): lax.ppermute(value, axis, [(source, source + steps) for source in range(i...  356 us
    reduce_scatter x1, waiting for transfers between devices, shards(): lax.psum_scatter((jnp.concatenate([left_part, right_part], axis=1) * live...  147 us
    all_gather x1, waiting for transfers between devices, shards(): lax.all_gather(w_in[0], 'dp', axis=0, tiled=True)  62 us
    all_gather x1, waiting for transfers between devices, shards(): lax.all_gather(w_out[0], 'dp', axis=0, tiled=True)  39.4 us
    dynamic_update_slice x76, other arithmetic, store(): lax.dynamic_update_index_in_dim(buffer, jnp.where(active, value, older),...  26.2 us
    ppermute x19, starting transfers between devices, shifted(): lax.ppermute(value, axis, [(source, source + steps) for source in range(i...  24.5 us
    dot_general x4, matrix products, retention_back(): jnp.dot(inputs, weight_in, preferred_element_type=jnp.float32)  22.1 us
  transfers between devices with their start and end apart: 22, of which 22 were waited for; matrix products, arithmetic and copies ran while one was open for 1% of the time, Pallas kernels for 0%

commit v1 on v0

v1 whole, which is shorter than its diff:
```python
import functools

import jax
import jax.numpy as jnp
from jax import lax
from jax.experimental import pallas as pl
from jax.experimental.pallas import tpu as pltpu
from jax.sharding import PartitionSpec as P

MESH = pl.DeviceIdType.MESH
BF = jnp.bfloat16
F32 = jnp.float32


def dot(a, b):
    return jnp.dot(a, b, preferred_element_type=F32)


def dot_nt(a, b):
    return lax.dot_general(a, b, (((1,), (1,)), ((), ())), preferred_element_type=F32)


def dot_tn(a, b):
    return lax.dot_general(a, b, (((0,), (0,)), ((), ())), preferred_element_type=F32)


def kernel(
    dims,
    acts, out_grad, w_in, w_out, rates, order,
    in_grad, grad_in, grad_out,
    WI, WO, XB, DY, NX, ACC, QKV, SC, DR, TAB, XS, DS, DQ, RA, GI, GO,
    loc, wsend, wrecv, csend, crecv, xsend, xrecv, rsend, rrecv, qsend, qrecv, ysend, yrecv, outsem,
):
    nsec, ndp, micro, tok, width, heads, hd, nchunk = dims
    cols = heads * hd
    blk = width // ndp
    half = blk // 2
    per = ndp // nchunk
    nx = ndp // 4
    s = lax.axis_index("section")
    r = lax.axis_index("dp")
    x, zl, c = r // 4, (r // 2) % 2, r % 2
    last = nsec - 1
    slot = c * (ndp // 2) + r // 2

    def rep(xx, zz, cc):
        return lax.rem(xx + nx, nx) * 4 + zz * 2 + cc

    core, zp = rep(x, zl, 1 - c), rep(x, 1 - zl, c)
    xp, xm, xo = rep(x + 1, zl, c), rep(x - 1, zl, c), rep(x + 2, zl, c)
    xpz, xmz, xoz = rep(x + 1, 1 - zl, c), rep(x - 1, 1 - zl, c), rep(x + 2, 1 - zl, c)

    def peer(i):
        return lax.rem(r + i, ndp)

    def slot_of(q):
        return lax.rem(q, 2) * (ndp // 2) + q // 2

    local = [
        pltpu.make_async_copy(w_in.at[0], WI.at[r], loc.at[0]),
        pltpu.make_async_copy(w_out.at[0], WO.at[r], loc.at[1]),
    ]
    for i in range(ndp):
        local.append(
            pltpu.make_async_copy(
                acts.at[0, :, :, pl.ds(i * blk, blk)], XB.at[i], loc.at[2 + i]
            )
        )
    for copy in local:
        copy.start()

    barrier = pltpu.get_barrier_semaphore()
    for i in range(1, ndp):
        pl.semaphore_signal(barrier, inc=1, device_id=(s, peer(i)), device_id_type=MESH)

    @pl.when(s > 0)
    def _():
        pl.semaphore_signal(barrier, inc=1, device_id=(s - 1, r), device_id_type=MESH)

    @pl.when(s < last)
    def _():
        pl.semaphore_signal(barrier, inc=1, device_id=(s + 1, r), device_id_type=MESH)

    neighbours = jnp.where(s > 0, 1, 0) + jnp.where(s < last, 1, 0)
    pl.semaphore_wait(barrier, ndp - 1 + neighbours)

    def piece(ref, q, h):
        return ref.at[q, pl.ds(h * half, half)]

    sent = []

    def push(q, h, target, own=False):
        for which, ref in enumerate((WI, WO)):
            if own:
                src = (w_in, w_out)[which].at[0, pl.ds(h * half, half)]
            else:
                src = piece(ref, q, h)
            copy = pltpu.make_async_remote_copy(
                src_ref=src,
                dst_ref=piece(ref, q, h),
                send_sem=wsend.at[len(sent)],
                recv_sem=wrecv.at[q, h, which],
                device_id=(s, target),
                device_id_type=MESH,
            )
            copy.start()
            sent.append(copy)

    def arrive(q, h):
        for which, ref in enumerate((WI, WO)):
            pltpu.make_async_remote_copy(
                src_ref=piece(ref, q, h),
                dst_ref=piece(ref, q, h),
                send_sem=wsend.at[0],
                recv_sem=wrecv.at[q, h, which],
                device_id=(s, core),
                device_id_type=MESH,
            ).wait_recv()

    for h in range(2):
        for target in (xp, xm, zp, core):
            push(r, h, target, own=True)

    ACC[...] = jnp.zeros_like(ACC)

    def add(q):
        ACC[...] += dot(XB[q].reshape(micro * tok, blk), WI[q])

    for copy in local:
        copy.wait()

    @pl.when(s == last)
    def _():
        for i in range(ndp):
            pltpu.make_async_copy(
                out_grad.at[:, :, pl.ds(i * blk, blk)], DY.at[:, i], outsem.at[i]
            ).start()

    spot_t = lax.broadcasted_iota(jnp.int32, (tok, tok), 0)
    spot_j = lax.broadcasted_iota(jnp.int32, (tok, tok), 1)
    offset = (spot_t - spot_j).astype(F32)
    for h in range(heads):
        decayed = jnp.exp(-rates[0, h] * jnp.maximum(offset, 0.0))
        TAB[h] = jnp.where(offset >= 0.0, decayed, 0.0)

    add(r)
    arrive(xm, 0)
    push(xm, 0, xp)
    push(xm, 0, core)
    arrive(xp, 0)
    push(xp, 0, core)
    arrive(zp, 0)
    push(zp, 0, xp)
    push(zp, 0, xm)
    push(zp, 0, core)
    arrive(core, 0)
    arrive(core, 1)
    add(core)
    arrive(xp, 1)
    push(xp, 1, xm)
    push(xp, 1, core)
    arrive(xm, 1)
    push(xm, 1, core)
    arrive(zp, 1)
    push(zp, 1, xp)
    push(zp, 1, xm)
    push(zp, 1, core)
    add(xm)
    add(xp)
    add(zp)
    arrive(xo, 0)
    push(xo, 0, zp)
    push(xo, 0, core)
    arrive(xo, 1)
    push(xo, 1, zp)
    push(xo, 1, core)

    def other(q):
        return q + 1 - 2 * c

    for q in (xm, xp, zp):
        arrive(other(q), 0)
        arrive(other(q), 1)
        add(other(q))
    add(xo)
    for q in (xmz, xpz):
        for h in range(2):
            arrive(q, h)
            push(q, h, core)
    arrive(xoz, 0)
    push(xoz, 0, core)
    add(xmz)
    add(xpz)
    arrive(xoz, 1)
    push(xoz, 1, core)
    for q in (xo, xmz, xpz):
        arrive(other(q), 0)
        arrive(other(q), 1)
        add(other(q))
    add(xoz)
    arrive(other(xoz), 0)
    arrive(other(xoz), 1)
    add(other(xoz))

    failed = order[ndp - 1]
    live = jnp.where(r == failed, 0.0, 1.0).astype(F32)
    mine = pl.ds(pl.multiple_of(slot * tok, tok), tok)

    QKV[...] = ACC[...].astype(BF).reshape(micro, tok, 3 * cols)
    for m in range(micro):
        for h in range(heads):
            q = QKV[m, :, h * hd : (h + 1) * hd]
            k = QKV[m, :, cols + h * hd : cols + (h + 1) * hd]
            v = QKV[m, :, 2 * cols + h * hd : 2 * cols + (h + 1) * hd]
            score = (dot_nt(q, k) * TAB[h] / hd).astype(BF)
            SC[m, h] = score
            mixed = dot(score, v).astype(BF)
            RA[m, mine, h * hd : (h + 1) * hd] = (mixed.astype(F32) * live).astype(BF)

    plane = pl.ds(pl.multiple_of(c * (ndp // 2) * tok, tok), (ndp // 2) * tok)
    foreign = pl.ds(pl.multiple_of((1 - c) * (ndp // 2) * tok, tok), (ndp // 2) * tok)

    def rows_of(q):
        return pl.ds(pl.multiple_of(slot_of(q) * tok, tok), tok)

    def x_copy(i):
        q = peer(i)
        return pltpu.make_async_remote_copy(
            src_ref=XB.at[q], dst_ref=XS.at[:, mine],
            send_sem=xsend.at[i], recv_sem=xrecv.at[i],
            device_id=(s, q), device_id_type=MESH,
        )

    def x_wait(i):
        q = lax.rem(r - i + ndp, ndp)
        pltpu.make_async_remote_copy(
            src_ref=XB.at[q], dst_ref=XS.at[:, rows_of(q)],
            send_sem=xsend.at[i], recv_sem=xrecv.at[i],
            device_id=(s, q), device_id_type=MESH,
        ).wait_recv()

    def r_copy(i):
        q = peer(2 * i)
        return pltpu.make_async_remote_copy(
            src_ref=RA.at[:, mine], dst_ref=RA.at[:, mine],
            send_sem=rsend.at[i], recv_sem=rrecv.at[i],
            device_id=(s, q), device_id_type=MESH,
        )

    def r_wait(i):
        q = lax.rem(r - 2 * i + ndp, ndp)
        pltpu.make_async_remote_copy(
            src_ref=RA.at[:, rows_of(q)], dst_ref=RA.at[:, rows_of(q)],
            send_sem=rsend.at[i], recv_sem=rrecv.at[i],
            device_id=(s, q), device_id_type=MESH,
        ).wait_recv()

    def r_swap(rows):
        return pltpu.make_async_remote_copy(
            src_ref=RA.at[:, rows], dst_ref=RA.at[:, rows],
            send_sem=rsend.at[0], recv_sem=rrecv.at[0],
            device_id=(s, core), device_id_type=MESH,
        )

    own_x = pltpu.make_async_copy(XB.at[r], XS.at[:, mine], loc.at[0])

    def exchange_early():
        for i in range(1, ndp // 2):
            r_copy(i).start()
        own_x.start()
        for i in range(1, ndp):
            x_copy(i).start()
        for i in range(1, ndp // 2):
            r_wait(i)
        r_swap(plane).start()

    pl.when(s < last)(exchange_early)

    def chunk_copy(m, k):
        part = pl.ds(k * per, per)
        return pltpu.make_async_remote_copy(
            src_ref=NX.at[m, part], dst_ref=DY.at[m, part],
            send_sem=csend.at[m, k], recv_sem=crecv.at[m, k],
            device_id=(jnp.maximum(s - 1, 0), r), device_id_type=MESH,
        )

    def q_copy(m, i):
        q = peer(2 * i)
        return pltpu.make_async_remote_copy(
            src_ref=DQ.at[m, mine], dst_ref=DQ.at[m, mine],
            send_sem=qsend.at[m, i], recv_sem=qrecv.at[m, i],
            device_id=(s, q), device_id_type=MESH,
        )

    def q_wait(m, i):
        q = lax.rem(r - 2 * i + ndp, ndp)
        pltpu.make_async_remote_copy(
            src_ref=DQ.at[m, rows_of(q)], dst_ref=DQ.at[m, rows_of(q)],
            send_sem=qsend.at[m, i], recv_sem=qrecv.at[m, i],
            device_id=(s, q), device_id_type=MESH,
        ).wait_recv()

    def q_swap(m, rows):
        return pltpu.make_async_remote_copy(
            src_ref=DQ.at[m, rows], dst_ref=DQ.at[m, rows],
            send_sem=qsend.at[m, 0], recv_sem=qrecv.at[m, 0],
            device_id=(s, core), device_id_type=MESH,
        )

    def y_copy(m, i):
        q = peer(i)
        return pltpu.make_async_remote_copy(
            src_ref=DY.at[m, q], dst_ref=DS.at[m, mine],
            send_sem=ysend.at[m, i], recv_sem=yrecv.at[m, i],
            device_id=(s, q), device_id_type=MESH,
        )

    def y_wait(m, i):
        q = lax.rem(r - i + ndp, ndp)
        pltpu.make_async_remote_copy(
            src_ref=DY.at[m, q], dst_ref=DS.at[m, rows_of(q)],
            send_sem=ysend.at[m, i], recv_sem=yrecv.at[m, i],
            device_id=(s, q), device_id_type=MESH,
        ).wait_recv()

    @pl.when(s == last)
    def _():
        for i in range(ndp):
            pltpu.make_async_copy(
                out_grad.at[:, :, pl.ds(i * blk, blk)], DY.at[:, i], outsem.at[i]
            ).wait()

    def step(m, carry):
        d_mixed = jnp.zeros((tok, cols), F32)
        for k in range(nchunk):
            @pl.when(s < last)
            def _():
                chunk_copy(m, k).wait_recv()

            for j in range(k * per, (k + 1) * per):
                d_mixed += dot(DY[m, j], WO[j])
        d_mixed = d_mixed.astype(BF)
        parts = [[], [], []]
        for h in range(heads):
            q = QKV[m, :, h * hd : (h + 1) * hd]
            k = QKV[m, :, cols + h * hd : cols + (h + 1) * hd]
            v = QKV[m, :, 2 * cols + h * hd : 2 * cols + (h + 1) * hd]
            dr = d_mixed[:, h * hd : (h + 1) * hd]
            d_score = (dot_nt(dr, v) * TAB[h] / hd).astype(BF)
            parts[0].append(dot(d_score, k).astype(BF))
            parts[1].append(dot_tn(d_score, q).astype(BF))
            parts[2].append(dot_tn(SC[m, h], dr).astype(BF))
        d_all = jnp.concatenate(parts[0] + parts[1] + parts[2], axis=1)
        for k in range(nchunk):
            for j in range(k * per, (k + 1) * per):
                back = dot_nt(d_all, WI[j])
                NX[m, j] = (DY[m, j].astype(F32) + back).astype(BF)

            @pl.when(s > 0)
            def _():
                chunk_copy(m, k).start()

        DQ[m, mine] = (d_all.astype(F32) * live).astype(BF)
        for i in range(1, ndp // 2):
            q_copy(m, i).start()
        DS[m, mine] = DY[m, r]
        for i in range(1, ndp):
            y_copy(m, i).start()

        @pl.when(m > 0)
        def _():
            for i in range(1, ndp // 2):
                q_wait(m - 1, i)
            q_swap(m - 1, plane).start()

        return carry

    lax.fori_loop(0, micro, step, 0)
    write = pltpu.make_async_copy(NX, in_grad, outsem.at[0])
    write.start()

    pl.when(s == last)(exchange_early)

    for i in range(1, ndp):
        x_wait(i)
    own_x.wait()
    r_swap(foreign).wait_recv()
    scale = 1.0 / (ndp - 2 + 1.0)
    for m in range(micro - 1):
        q_swap(m, foreign).wait_recv()
        for i in range(1, ndp):
            y_wait(m, i)
        if m == 0:
            GI[...] = dot_tn(XS[m], DQ[m])
            GO[...] = dot_tn(DS[m], RA[m])
        else:
            GI[...] += dot_tn(XS[m], DQ[m])
            GO[...] += dot_tn(DS[m], RA[m])
    m = micro - 1
    for i in range(1, ndp // 2):
        q_wait(m, i)
    q_swap(m, plane).start()
    for i in range(1, ndp):
        y_wait(m, i)
    GO[...] = (GO[...] + dot_tn(DS[m], RA[m])) * scale
    out1 = pltpu.make_async_copy(GO, grad_out.at[0], outsem.at[1])
    out1.start()
    q_swap(m, foreign).wait_recv()
    GI[...] = (GI[...] + dot_tn(XS[m], DQ[m])) * scale
    out2 = pltpu.make_async_copy(GI, grad_in.at[0], outsem.at[2])
    out2.start()

    for copy in sent:
        copy.wait_send()
    for i in range(1, ndp):
        x_copy(i).wait_send()
    for i in range(1, ndp // 2):
        r_copy(i).wait_send()
    r_swap(plane).wait_send()

    def drain(m, carry):
        @pl.when(s > 0)
        def _():
            for k in range(nchunk):
                chunk_copy(m, k).wait_send()

        for i in range(1, ndp // 2):
            q_copy(m, i).wait_send()
        q_swap(m, plane).wait_send()
        for i in range(1, ndp):
            y_copy(m, i).wait_send()
        return carry

    lax.fori_loop(0, micro, drain, 0)
    write.wait()
    out1.wait()
    out2.wait()


def shards(acts, out_grad, w_in, w_out, decay_rate, cycle_order):
    nsec = lax.axis_size("section")
    ndp = lax.axis_size("dp")
    _, micro, tok, width = acts.shape
    cols = w_out.shape[2]
    heads = decay_rate.shape[1]
    hd = cols // heads
    blk = width // ndp
    nchunk = 4
    dims = (nsec, ndp, micro, tok, width, heads, hd, nchunk)
    dma = pltpu.SemaphoreType.DMA
    any_spec = pl.BlockSpec(memory_space=pl.ANY)
    smem = pl.BlockSpec(memory_space=pltpu.SMEM)
    in_grad, grad_in, grad_out = pl.pallas_call(
        functools.partial(kernel, dims),
        name="retention_stack_back",
        out_shape=(
            jax.ShapeDtypeStruct((micro, ndp, tok, blk), BF),
            jax.ShapeDtypeStruct((1, blk, 3 * cols), F32),
            jax.ShapeDtypeStruct((1, blk, cols), F32),
        ),
        in_specs=[any_spec] * 4 + [smem] * 2,
        out_specs=[any_spec] * 3,
        scratch_shapes=[
            pltpu.VMEM((ndp, blk, 3 * cols), BF),
            pltpu.VMEM((ndp, blk, cols), BF),
            pltpu.VMEM((ndp, micro, tok, blk), BF),
            pltpu.VMEM((micro, ndp, tok, blk), BF),
            pltpu.VMEM((micro, ndp, tok, blk), BF),
            pltpu.VMEM((micro * tok, 3 * cols), F32),
            pltpu.VMEM((micro, tok, 3 * cols), BF),
            pltpu.VMEM((micro, heads, tok, tok), BF),
            pltpu.VMEM((tok, cols), F32),
            pltpu.VMEM((heads, tok, tok), F32),
            pltpu.VMEM((micro, ndp * tok, blk), BF),
            pltpu.VMEM((micro, ndp * tok, blk), BF),
            pltpu.VMEM((micro, ndp * tok, 3 * cols), BF),
            pltpu.VMEM((micro, ndp * tok, cols), BF),
            pltpu.VMEM((blk, 3 * cols), F32),
            pltpu.VMEM((blk, cols), F32),
            dma((2 + ndp,)),
            dma((64,)),
            dma((ndp, 2, 2)),
            dma((micro, nchunk)),
            dma((micro, nchunk)),
            dma((ndp,)),
            dma((ndp,)),
            dma((ndp // 2,)),
            dma((ndp // 2,)),
            dma((micro, ndp // 2)),
            dma((micro, ndp // 2)),
            dma((micro, ndp)),
            dma((micro, ndp)),
            dma((ndp,)),
        ],
        compiler_params=pltpu.CompilerParams(
            collective_id=0, has_side_effects=True, vmem_limit_bytes=60 * 1024 * 1024
        ),
        cost_estimate=pl.CostEstimate(
            flops=6_000_000_000, bytes_accessed=8_000_000, transcendentals=4096
        ),
    )(acts, out_grad, w_in, w_out, decay_rate, cycle_order)
    in_grad = jnp.swapaxes(in_grad, 1, 2).reshape(1, micro, tok, width)
    return (in_grad, grad_in, grad_out)


def solution(mesh):
    placed = (
        P("section", None, "dp", None),
        P(None, "dp", None),
        P("section", "dp", None),
        P("section", "dp", None),
        P("section", None),
        P(),
    )
    return jax.shard_map(
        shards,
        mesh=mesh,
        in_specs=placed,
        out_specs=(
            P("section", None, "dp", None),
            P("section", "dp", None),
            P("section", "dp", None),
        ),
        check_vma=False,
    )
```

time: 767 us -> 265 us (0.35)
  waiting for transfers between devices: 606 us -> 0 us
  Pallas kernels: 0 us -> 258 us
  matrix products: 55.9 us -> 0 us
  other arithmetic: 37.4 us -> 0 us
  starting transfers between devices: 24.7 us -> 0 us
  local copies, waits for them, and re-layouts: 22.7 us -> 5.22 us
  between operations: 14.5 us -> 0.65 us
    ppermute x19 -> x0, waiting for transfers between devices: 356 us -> none  [shifted(): lax.ppermute(value, axis, [(source, source + steps) for source in range(i...]
    pallas_call x0 -> x1, Pallas kernels: none -> 258 us  [shards(): pl.pallas_call(functools.partial(kernel, dims), name='retention_stack_bac...]
    reduce_scatter x1 -> x0, waiting for transfers between devices: 147 us -> none  [shards(): lax.psum_scatter((jnp.concatenate([left_part, right_part], axis=1) * live...]
    all_gather x2 -> x0, waiting for transfers between devices: 101 us -> none  [the longest x1 62 us: shards(): lax.all_gather(w_in[0], 'dp', axis=0, tiled=True)]
    dot_general x38 -> x0, matrix products: 55.9 us -> none  [the longest x4 22.1 us: retention_back(): jnp.dot(inputs, weight_in, preferred_element_type=jnp.float32)]
    dynamic_update_slice x76 -> x0, other arithmetic: 26.2 us -> none  [store(): lax.dynamic_update_index_in_dim(buffer, jnp.where(active, value, older),...]
    ppermute x19 -> x0, starting transfers between devices: 24.5 us -> none  [shifted(): lax.ppermute(value, axis, [(source, source + steps) for source in range(i...]
    convert_element_type x3 -> x0, other arithmetic: 10.3 us -> none  [the longest x1 9.04 us: shards(): (jnp.concatenate([left_part, right_part], axis=1) * live).astype(jnp.bflo...]
  transfers between devices with their start and end apart: 22 -> 0, of which waited for: 22 -> 0; matrix products, arithmetic and copies ran while one was open for 1% -> 0% of each run, Pallas kernels for 0% -> 0%
where the time goes in v1:
time: 265 us; the launch traced here: 264 us
  Pallas kernels  258 us (97%)
  local copies, waits for them, and re-layouts  5.22 us (2%)
    pallas_call x1, Pallas kernels, shards(): pl.pallas_call(functools.partial(kernel, dims), name='retention_stack_bac...  258 us

profile of v1, /device:TPU:33, one launch (start us, length us, event | category | flops | bytes accessed | tf_op | source)
XLA Modules:
  0.0 263.6 jit_solution(10874072694149118202)
XLA Ops:
  0.6 257.7 %retention_stack_back.1 = (bf16[4,16,32,256]{3,2,1,0:T(8,128)(2,1)}, f32[1,256,1152]{2,1,0:T(8,128)}, f32[1,256,384]{2,1,0:T(8,128)}) custom-call(bf16[1,4,32,4096]{3,2,1,0:T(8,128)(2,1)} %acts.1, bf16[4,32,4096]{2,1,0:T(8,128)(2,1)} %out_grad.1, bf16[1,256,1152]{2,1,0:T(8,128)(2,1)} %w_in.1, bf16[1,256,384]{2,1,0:T(8,128)(2,1)} %w_out.1, f32[1,3]{1,0:T(1,128)} %rates.1, ...), custom_call_target="tpu_custom_call" | custom-call | flops 6000000000 | bytes 8000000 | tf_op jit(solution)/shard_map/retention_stack_back/pallas_call | solution.py:453
  258.4 1.8 copy.9
  260.2 0.0 copy-start
  260.2 1.3 reshape.9
  261.5 0.1 copy-done
  261.6 0.0 copy-start.1
  261.6 1.0 copy.12
  262.7 0.2 copy-done.1
  262.9 0.7 copy.13
Async XLA Ops:
  260.2 1.4 copy-start
  261.6 1.2 copy-start.1

commit v2 on v1

--- a/solution.py
+++ b/solution.py
@@ -28,7 +28,7 @@
     dims,
     acts, out_grad, w_in, w_out, rates, order,
     in_grad, grad_in, grad_out,
-    WI, WO, XB, DY, NX, ACC, QKV, SC, DR, TAB, XS, DS, DQ, RA, GI, GO,
+    WI, WO, WT, XB, DY, NX, ACC, QKV, SC, TAB, XS, DS, DQ, RA, GI, GO,
     loc, wsend, wrecv, csend, crecv, xsend, xrecv, rsend, rrecv, qsend, qrecv, ysend, yrecv, outsem,
 ):
     nsec, ndp, micro, tok, width, heads, hd, nchunk = dims
@@ -41,6 +41,7 @@
     r = lax.axis_index("dp")
     x, zl, c = r // 4, (r // 2) % 2, r % 2
     last = nsec - 1
+    lead = min(4, nsec // 4)
     slot = c * (ndp // 2) + r // 2
 
     def rep(xx, zz, cc):
@@ -125,6 +126,7 @@
 
     def add(q):
         ACC[...] += dot(XB[q].reshape(micro * tok, blk), WI[q])
+        WT[q] = WI[q].T
 
     for copy in local:
         copy.wait()
@@ -273,8 +275,15 @@
         for i in range(1, ndp // 2):
             r_wait(i)
         r_swap(plane).start()
-
-    pl.when(s < last)(exchange_early)
+        own_x.wait()
+        for i in range(1, ndp):
+            x_wait(i)
+        r_swap(foreign).wait_recv()
+
+    GI[...] = jnp.zeros_like(GI)
+    GO[...] = jnp.zeros_like(GO)
+    early = s < last - lead
+    pl.when(early)(exchange_early)
 
     def chunk_copy(m, k):
         part = pl.ds(k * per, per)
@@ -329,6 +338,13 @@
             pltpu.make_async_copy(
                 out_grad.at[:, :, pl.ds(i * blk, blk)], DY.at[:, i], outsem.at[i]
             ).wait()
+
+    def settle(m):
+        q_swap(m, foreign).wait_recv()
+        for i in range(1, ndp):
+            y_wait(m, i)
+        GI[...] += dot_tn(XS[m], DQ[m])
+        GO[...] += dot_tn(DS[m], RA[m])
 
     def step(m, carry):
         d_mixed = jnp.zeros((tok, cols), F32)
@@ -353,7 +369,7 @@
         d_all = jnp.concatenate(parts[0] + parts[1] + parts[2], axis=1)
         for k in range(nchunk):
             for j in range(k * per, (k + 1) * per):
-                back = dot_nt(d_all, WI[j])
+                back = dot(d_all, WT[j])
                 NX[m, j] = (DY[m, j].astype(F32) + back).astype(BF)
 
             @pl.when(s > 0)
@@ -373,29 +389,32 @@
                 q_wait(m - 1, i)
             q_swap(m - 1, plane).start()
 
+        @pl.when((m > 1) & early)
+        def _():
+            settle(m - 2)
+
         return carry
 
     lax.fori_loop(0, micro, step, 0)
-    write = pltpu.make_async_copy(NX, in_grad, outsem.at[0])
-    write.start()
-
-    pl.when(s == last)(exchange_early)
-
-    for i in range(1, ndp):
-        x_wait(i)
-    own_x.wait()
-    r_swap(foreign).wait_recv()
-    scale = 1.0 / (ndp - 2 + 1.0)
-    for m in range(micro - 1):
-        q_swap(m, foreign).wait_recv()
-        for i in range(1, ndp):
-            y_wait(m, i)
-        if m == 0:
-            GI[...] = dot_tn(XS[m], DQ[m])
-            GO[...] = dot_tn(DS[m], RA[m])
-        else:
-            GI[...] += dot_tn(XS[m], DQ[m])
-            GO[...] += dot_tn(DS[m], RA[m])
+    writes = [
+        pltpu.make_async_copy(
+            NX.at[:, i], in_grad.at[0, :, :, pl.ds(i * blk, blk)], outsem.at[i]
+        )
+        for i in range(ndp)
+    ]
+    for copy in writes:
+        copy.start()
+
+    pl.when(s >= last - lead)(exchange_early)
+
+    scale = 1.0 / (ndp - 1.0)
+
+    @pl.when(s >= last - lead)
+    def _():
+        for m in range(micro - 2):
+            settle(m)
+
+    settle(micro - 2)
     m = micro - 1
     for i in range(1, ndp // 2):
         q_wait(m, i)
@@ -403,11 +422,11 @@
     for i in range(1, ndp):
         y_wait(m, i)
     GO[...] = (GO[...] + dot_tn(DS[m], RA[m])) * scale
-    out1 = pltpu.make_async_copy(GO, grad_out.at[0], outsem.at[1])
+    out1 = pltpu.make_async_copy(GO, grad_out.at[0], loc.at[1])
     out1.start()
     q_swap(m, foreign).wait_recv()
     GI[...] = (GI[...] + dot_tn(XS[m], DQ[m])) * scale
-    out2 = pltpu.make_async_copy(GI, grad_in.at[0], outsem.at[2])
+    out2 = pltpu.make_async_copy(GI, grad_in.at[0], loc.at[2])
     out2.start()
 
     for copy in sent:
@@ -432,7 +451,8 @@
         return carry
 
     lax.fori_loop(0, micro, drain, 0)
-    write.wait()
+    for copy in writes:
+        copy.wait()
     out1.wait()
     out2.wait()
 
@@ -450,11 +470,11 @@
     dma = pltpu.SemaphoreType.DMA
     any_spec = pl.BlockSpec(memory_space=pl.ANY)
     smem = pl.BlockSpec(memory_space=pltpu.SMEM)
-    in_grad, grad_in, grad_out = pl.pallas_call(
+    return pl.pallas_call(
         functools.partial(kernel, dims),
         name="retention_stack_back",
         out_shape=(
-            jax.ShapeDtypeStruct((micro, ndp, tok, blk), BF),
+            jax.ShapeDtypeStruct((1, micro, tok, width), BF),
             jax.ShapeDtypeStruct((1, blk, 3 * cols), F32),
             jax.ShapeDtypeStruct((1, blk, cols), F32),
         ),
@@ -463,13 +483,13 @@
         scratch_shapes=[
             pltpu.VMEM((ndp, blk, 3 * cols), BF),
             pltpu.VMEM((ndp, blk, cols), BF),
+            pltpu.VMEM((ndp, 3 * cols, blk), BF),
             pltpu.VMEM((ndp, micro, tok, blk), BF),
             pltpu.VMEM((micro, ndp, tok, blk), BF),
             pltpu.VMEM((micro, ndp, tok, blk), BF),
             pltpu.VMEM((micro * tok, 3 * cols), F32),
             pltpu.VMEM((micro, tok, 3 * cols), BF),
             pltpu.VMEM((micro, heads, tok, tok), BF),
-            pltpu.VMEM((tok, cols), F32),
             pltpu.VMEM((heads, tok, tok), F32),
             pltpu.VMEM((micro, ndp * tok, blk), BF),
             pltpu.VMEM((micro, ndp * tok, blk), BF),
@@ -499,8 +519,6 @@
             flops=6_000_000_000, bytes_accessed=8_000_000, transcendentals=4096
         ),
     )(acts, out_grad, w_in, w_out, decay_rate, cycle_order)
-    in_grad = jnp.swapaxes(in_grad, 1, 2).reshape(1, micro, tok, width)
-    return (in_grad, grad_in, grad_out)
 
 
 def solution(mesh):

time: 265 us -> 256 us (0.966)
  Pallas kernels: 258 us -> 248 us
    pallas_call x1, Pallas kernels: 258 us -> 248 us  [shards(): pl.pallas_call(functools.partial(kernel, dims), name='retention_stack_bac...]
where the time goes in v2:
time: 256 us; the launch traced here: 253 us
  Pallas kernels  248 us (97%)
  local copies, waits for them, and re-layouts  4.36 us (2%)
    pallas_call x1, Pallas kernels, shards(): pl.pallas_call(functools.partial(kernel, dims), name='retention_stack_bac...  248 us

profile of v2, /device:TPU:33, one launch (start us, length us, event | category | flops | bytes accessed | tf_op | source)
XLA Modules:
  0.0 253.3 jit_solution(15906224059494807840)
XLA Ops:
  0.6 248.3 %retention_stack_back.1 = (bf16[1,4,32,4096]{3,2,1,0:T(8,128)(2,1)}, f32[1,256,1152]{2,1,0:T(8,128)}, f32[1,256,384]{2,1,0:T(8,128)}) custom-call(bf16[1,4,32,4096]{3,2,1,0:T(8,128)(2,1)} %acts.1, bf16[4,32,4096]{2,1,0:T(8,128)(2,1)} %out_grad.1, bf16[1,256,1152]{2,1,0:T(8,128)(2,1)} %w_in.1, bf16[1,256,384]{2,1,0:T(8,128)(2,1)} %w_out.1, f32[1,3]{1,0:T(1,128)} %rates.1, ...), custom_call_target="tpu_custom_call" | custom-call | flops 6000000000 | bytes 8000000 | tf_op jit(solution)/shard_map/retention_stack_back/pallas_call | solution.py:473
  248.9 0.0 copy-start
  249.0 2.4 copy.12
  251.3 0.0 copy-done
  251.3 0.0 copy-start.1
  251.3 1.0 copy.13
  252.4 0.2 copy-done.1
  252.6 0.7 copy.14
Async XLA Ops:
  248.9 2.4 copy-start
  251.3 1.2 copy-start.1

commit v3 on v2

--- a/solution.py
+++ b/solution.py
@@ -28,8 +28,8 @@
     dims,
     acts, out_grad, w_in, w_out, rates, order,
     in_grad, grad_in, grad_out,
-    WI, WO, WT, XB, DY, NX, ACC, QKV, SC, TAB, XS, DS, DQ, RA, GI, GO,
-    loc, wsend, wrecv, csend, crecv, xsend, xrecv, rsend, rrecv, qsend, qrecv, ysend, yrecv, outsem,
+    WI, WO, WT, XB, DY, NX, RB, ACC, QKV, SC, TAB, XS, DS, DQ, RA, GI, GO,
+    loc, wsend, wrecv, csend, crecv, bsend, brecv, xsend, xrecv, rsend, rrecv, qsend, qrecv, ysend, yrecv, outsem,
 ):
     nsec, ndp, micro, tok, width, heads, hd, nchunk = dims
     cols = heads * hd
@@ -42,6 +42,13 @@
     x, zl, c = r // 4, (r // 2) % 2, r % 2
     last = nsec - 1
     lead = min(4, nsec // 4)
+    ny = 4 if nsec >= 16 else 2
+    y = lax.rem(s, ny)
+    to_relay = (s > 0) & (y == 0) & (zl == 0)
+    to_next = (s > 0) & ((y != 0) | (zl != 0))
+    node = (s >= ny) & (y == ny - 1) & (zl == 0)
+    by_relay = (s < last) & (y == ny - 1) & (zl == 0)
+    by_prev = (s < last) & ((y != ny - 1) | (zl != 0))
     slot = c * (ndp // 2) + r // 2
 
     def rep(xx, zz, cc):
@@ -74,16 +81,20 @@
     for i in range(1, ndp):
         pl.semaphore_signal(barrier, inc=1, device_id=(s, peer(i)), device_id_type=MESH)
 
-    @pl.when(s > 0)
-    def _():
-        pl.semaphore_signal(barrier, inc=1, device_id=(s - 1, r), device_id_type=MESH)
-
-    @pl.when(s < last)
-    def _():
-        pl.semaphore_signal(barrier, inc=1, device_id=(s + 1, r), device_id_type=MESH)
-
-    neighbours = jnp.where(s > 0, 1, 0) + jnp.where(s < last, 1, 0)
-    pl.semaphore_wait(barrier, ndp - 1 + neighbours)
+    def greet(cond, section):
+        @pl.when(cond)
+        def _():
+            pl.semaphore_signal(
+                barrier, inc=1, device_id=(section, r), device_id_type=MESH
+            )
+
+    greet(by_prev, jnp.minimum(s + 1, last))
+    greet(by_relay, jnp.minimum(s + ny, last))
+    greet(node, jnp.maximum(s - (ny - 1), 0))
+    receivers = (
+        jnp.where(to_next, 1, 0) + jnp.where(to_relay, 1, 0) + jnp.where(node, 1, 0)
+    )
+    pl.semaphore_wait(barrier, ndp - 1 + receivers)
 
     def piece(ref, q, h):
         return ref.at[q, pl.ds(h * half, half)]
@@ -293,6 +304,22 @@
             device_id=(jnp.maximum(s - 1, 0), r), device_id_type=MESH,
         )
 
+    def relay_copy(m, k):
+        part = pl.ds(k * per, per)
+        return pltpu.make_async_remote_copy(
+            src_ref=NX.at[m, part], dst_ref=RB.at[m, part],
+            send_sem=csend.at[m, k], recv_sem=brecv.at[m, k],
+            device_id=(jnp.minimum(s + ny - 1, last), r), device_id_type=MESH,
+        )
+
+    def pass_on(m, k):
+        part = pl.ds(k * per, per)
+        return pltpu.make_async_remote_copy(
+            src_ref=RB.at[m, part], dst_ref=DY.at[m, part],
+            send_sem=bsend.at[m, k], recv_sem=crecv.at[m, k],
+            device_id=(jnp.maximum(s - ny, 0), r), device_id_type=MESH,
+        )
+
     def q_copy(m, i):
         q = peer(2 * i)
         return pltpu.make_async_remote_copy(
@@ -372,9 +399,13 @@
                 back = dot(d_all, WT[j])
                 NX[m, j] = (DY[m, j].astype(F32) + back).astype(BF)
 
-            @pl.when(s > 0)
+            @pl.when(to_next)
             def _():
                 chunk_copy(m, k).start()
+
+            @pl.when(to_relay)
+            def _():
+                relay_copy(m, k).start()
 
         DQ[m, mine] = (d_all.astype(F32) * live).astype(BF)
         for i in range(1, ndp // 2):
@@ -404,6 +435,16 @@
     ]
     for copy in writes:
         copy.start()
+
+    @pl.when(node)
+    def _():
+        def forward(m, carry):
+            for k in range(nchunk):
+                relay_copy(m, k).wait_recv()
+                pass_on(m, k).start()
+            return carry
+
+        lax.fori_loop(0, micro, forward, 0)
 
     pl.when(s >= last - lead)(exchange_early)
 
@@ -442,6 +483,11 @@
         def _():
             for k in range(nchunk):
                 chunk_copy(m, k).wait_send()
+
+        @pl.when(node)
+        def _():
+            for k in range(nchunk):
+                pass_on(m, k).wait_send()
 
         for i in range(1, ndp // 2):
             q_copy(m, i).wait_send()
@@ -487,6 +533,7 @@
             pltpu.VMEM((ndp, micro, tok, blk), BF),
             pltpu.VMEM((micro, ndp, tok, blk), BF),
             pltpu.VMEM((micro, ndp, tok, blk), BF),
+            pltpu.VMEM((micro, ndp, tok, blk), BF),
             pltpu.VMEM((micro * tok, 3 * cols), F32),
             pltpu.VMEM((micro, tok, 3 * cols), BF),
             pltpu.VMEM((micro, heads, tok, tok), BF),
@@ -500,6 +547,8 @@
             dma((2 + ndp,)),
             dma((64,)),
             dma((ndp, 2, 2)),
+            dma((micro, nchunk)),
+            dma((micro, nchunk)),
             dma((micro, nchunk)),
             dma((micro, nchunk)),
             dma((ndp,)),

time: 256 us -> 260 us (1.016)
  Pallas kernels: 248 us -> 254 us
    pallas_call x1, Pallas kernels: 248 us -> 254 us  [shards(): pl.pallas_call(functools.partial(kernel, dims), name='retention_stack_bac...]
where the time goes in v3:
time: 260 us; the launch traced here: 259 us
  Pallas kernels  254 us (98%)
  local copies, waits for them, and re-layouts  4.36 us (2%)
    pallas_call x1, Pallas kernels, shards(): pl.pallas_call(functools.partial(kernel, dims), name='retention_stack_bac...  254 us

profile of v3, /device:TPU:33, one launch (start us, length us, event | category | flops | bytes accessed | tf_op | source)
XLA Modules:
  0.0 258.7 jit_solution(4167710354380395661)
XLA Ops:
  0.6 253.6 %retention_stack_back.1 = (bf16[1,4,32,4096]{3,2,1,0:T(8,128)(2,1)}, f32[1,256,1152]{2,1,0:T(8,128)}, f32[1,256,384]{2,1,0:T(8,128)}) custom-call(bf16[1,4,32,4096]{3,2,1,0:T(8,128)(2,1)} %acts.1, bf16[4,32,4096]{2,1,0:T(8,128)(2,1)} %out_grad.1, bf16[1,256,1152]{2,1,0:T(8,128)(2,1)} %w_in.1, bf16[1,256,384]{2,1,0:T(8,128)(2,1)} %w_out.1, f32[1,3]{1,0:T(1,128)} %rates.1, ...), custom_call_target="tpu_custom_call" | custom-call | flops 6000000000 | bytes 8000000 | tf_op jit(solution)/shard_map/retention_stack_back/pallas_call | solution.py:519
  254.3 0.0 copy-start
  254.3 2.4 copy.12
  256.7 0.0 copy-done
  256.7 0.0 copy-start.1
  256.7 1.0 copy.13
  257.7 0.2 copy-done.1
  257.9 0.7 copy.14
Async XLA Ops:
  254.3 2.4 copy-start
  256.7 1.2 copy-start.1

commit v4 on v3

--- a/solution.py
+++ b/solution.py
@@ -373,6 +373,14 @@
         GI[...] += dot_tn(XS[m], DQ[m])
         GO[...] += dot_tn(DS[m], RA[m])
 
+    def exchange(m):
+        for i in range(1, ndp // 2):
+            q_copy(m, i).start()
+        for i in range(1, ndp):
+            y_copy(m, i).start()
+
+    inline = s < nsec // 3 + 1
+
     def step(m, carry):
         d_mixed = jnp.zeros((tok, cols), F32)
         for k in range(nchunk):
@@ -408,21 +416,11 @@
                 relay_copy(m, k).start()
 
         DQ[m, mine] = (d_all.astype(F32) * live).astype(BF)
-        for i in range(1, ndp // 2):
-            q_copy(m, i).start()
         DS[m, mine] = DY[m, r]
-        for i in range(1, ndp):
-            y_copy(m, i).start()
-
-        @pl.when(m > 0)
+
+        @pl.when(inline)
         def _():
-            for i in range(1, ndp // 2):
-                q_wait(m - 1, i)
-            q_swap(m - 1, plane).start()
-
-        @pl.when((m > 1) & early)
-        def _():
-            settle(m - 2)
+            exchange(m)
 
         return carry
 
@@ -448,18 +446,30 @@
 
     pl.when(s >= last - lead)(exchange_early)
 
+    @pl.when(s >= nsec // 3 + 1)
+    def _():
+        def send(m, carry):
+            exchange(m)
+            return carry
+
+        lax.fori_loop(0, micro, send, 0)
+
     scale = 1.0 / (ndp - 1.0)
 
-    @pl.when(s >= last - lead)
-    def _():
-        for m in range(micro - 2):
-            settle(m)
-
-    settle(micro - 2)
+    def swap(m):
+        for i in range(1, ndp // 2):
+            q_wait(m, i)
+        q_swap(m, plane).start()
+
+    swap(0)
+
+    def finish(m, carry):
+        swap(m + 1)
+        settle(m)
+        return carry
+
+    lax.fori_loop(0, micro - 1, finish, 0)
     m = micro - 1
-    for i in range(1, ndp // 2):
-        q_wait(m, i)
-    q_swap(m, plane).start()
     for i in range(1, ndp):
         y_wait(m, i)
     GO[...] = (GO[...] + dot_tn(DS[m], RA[m])) * scale

time: 260 us -> 251 us (0.965)
  Pallas kernels: 254 us -> 243 us
    pallas_call x1, Pallas kernels: 254 us -> 243 us  [shards(): pl.pallas_call(functools.partial(kernel, dims), name='retention_stack_bac...]
where the time goes in v4:
time: 251 us; the launch traced here: 249 us
  Pallas kernels  243 us (97%)
  local copies, waits for them, and re-layouts  4.36 us (2%)
    pallas_call x1, Pallas kernels, shards(): pl.pallas_call(functools.partial(kernel, dims), name='retention_stack_bac...  243 us

profile of v4, /device:TPU:33, one launch (start us, length us, event | category | flops | bytes accessed | tf_op | source)
XLA Modules:
  0.0 248.5 jit_solution(12868292888434835188)
XLA Ops:
  0.6 243.5 %retention_stack_back.1 = (bf16[1,4,32,4096]{3,2,1,0:T(8,128)(2,1)}, f32[1,256,1152]{2,1,0:T(8,128)}, f32[1,256,384]{2,1,0:T(8,128)}) custom-call(bf16[1,4,32,4096]{3,2,1,0:T(8,128)(2,1)} %acts.1, bf16[4,32,4096]{2,1,0:T(8,128)(2,1)} %out_grad.1, bf16[1,256,1152]{2,1,0:T(8,128)(2,1)} %w_in.1, bf16[1,256,384]{2,1,0:T(8,128)(2,1)} %w_out.1, f32[1,3]{1,0:T(1,128)} %rates.1, ...), custom_call_target="tpu_custom_call" | custom-call | flops 6000000000 | bytes 8000000 | tf_op jit(solution)/shard_map/retention_stack_back/pallas_call | solution.py:529
  244.1 0.0 copy-start
  244.1 2.4 copy.12
  246.5 0.0 copy-done
  246.5 0.0 copy-start.1
  246.5 1.0 copy.13
  247.5 0.2 copy-done.1
  247.8 0.7 copy.14
Async XLA Ops:
  244.1 2.4 copy-start
  246.5 1.2 copy-start.1

commit v5 on v4

--- a/solution.py
+++ b/solution.py
@@ -28,8 +28,8 @@
     dims,
     acts, out_grad, w_in, w_out, rates, order,
     in_grad, grad_in, grad_out,
-    WI, WO, WT, XB, DY, NX, RB, ACC, QKV, SC, TAB, XS, DS, DQ, RA, GI, GO,
-    loc, wsend, wrecv, csend, crecv, bsend, brecv, xsend, xrecv, rsend, rrecv, qsend, qrecv, ysend, yrecv, outsem,
+    WI, WS, WO, WT, MA, MM, DRB, DRN, RD, PA, XB, DY, NX, RB, ACC, QKV, SC, TAB, XS, DS, DQ, RA, GI, GO,
+    loc, wsend, wrecv, csend, crecv, bsend, brecv, dsend, drecv, esend, erecv, xsend, xrecv, rsend, rrecv, qsend, qrecv, ysend, yrecv, outsem,
 ):
     nsec, ndp, micro, tok, width, heads, hd, nchunk = dims
     cols = heads * hd
@@ -44,6 +44,8 @@
     lead = min(4, nsec // 4)
     ny = 4 if nsec >= 16 else 2
     y = lax.rem(s, ny)
+    direct = s >= last - 1
+    ahead = (s > 0) & (s < last)
     to_relay = (s > 0) & (y == 0) & (zl == 0)
     to_next = (s > 0) & ((y != 0) | (zl != 0))
     node = (s >= ny) & (y == ny - 1) & (zl == 0)
@@ -66,7 +68,7 @@
 
     local = [
         pltpu.make_async_copy(w_in.at[0], WI.at[r], loc.at[0]),
-        pltpu.make_async_copy(w_out.at[0], WO.at[r], loc.at[1]),
+        pltpu.make_async_copy(w_out.at[0], WS.at[r], loc.at[1]),
     ]
     for i in range(ndp):
         local.append(
@@ -91,8 +93,12 @@
     greet(by_prev, jnp.minimum(s + 1, last))
     greet(by_relay, jnp.minimum(s + ny, last))
     greet(node, jnp.maximum(s - (ny - 1), 0))
+    greet(ahead, jnp.maximum(s - 1, 0))
     receivers = (
-        jnp.where(to_next, 1, 0) + jnp.where(to_relay, 1, 0) + jnp.where(node, 1, 0)
+        jnp.where(to_next, 1, 0)
+        + jnp.where(to_relay, 1, 0)
+        + jnp.where(node, 1, 0)
+        + jnp.where(s < last - 1, 1, 0)
     )
     pl.semaphore_wait(barrier, ndp - 1 + receivers)
 
@@ -100,13 +106,14 @@
         return ref.at[q, pl.ds(h * half, half)]
 
     sent = []
-
-    def push(q, h, target, own=False):
-        for which, ref in enumerate((WI, WO)):
-            if own:
+    needed = (s >= 0, direct, ahead)
+
+    def push(q, h, target, arrays=(0, 1, 2), own=False):
+        for which in arrays:
+            ref = (WI, WS, WO)[which]
+            src = piece(ref, q, h)
+            if own and which < 2:
                 src = (w_in, w_out)[which].at[0, pl.ds(h * half, half)]
-            else:
-                src = piece(ref, q, h)
             copy = pltpu.make_async_remote_copy(
                 src_ref=src,
                 dst_ref=piece(ref, q, h),
@@ -115,29 +122,47 @@
                 device_id=(s, target),
                 device_id_type=MESH,
             )
-            copy.start()
-            sent.append(copy)
+            sent.append((copy, needed[which]))
+            pl.when(needed[which])(copy.start)
 
     def arrive(q, h):
-        for which, ref in enumerate((WI, WO)):
-            pltpu.make_async_remote_copy(
+        for which, ref in enumerate((WI, WS, WO)):
+            copy = pltpu.make_async_remote_copy(
                 src_ref=piece(ref, q, h),
                 dst_ref=piece(ref, q, h),
                 send_sem=wsend.at[0],
                 recv_sem=wrecv.at[q, h, which],
                 device_id=(s, core),
                 device_id_type=MESH,
-            ).wait_recv()
-
+            )
+            pl.when(needed[which])(copy.wait_recv)
+
+    def up_copy(h):
+        return pltpu.make_async_remote_copy(
+            src_ref=w_out.at[0, pl.ds(h * half, half)],
+            dst_ref=piece(WO, r, h),
+            send_sem=loc.at[2 + ndp + h],
+            recv_sem=wrecv.at[r, h, 2],
+            device_id=(jnp.minimum(s + 1, last), r),
+            device_id_type=MESH,
+        )
+
+    for h in range(2):
+        pl.when(s < last - 1)(up_copy(h).start)
     for h in range(2):
         for target in (xp, xm, zp, core):
-            push(r, h, target, own=True)
-
+            push(r, h, target, arrays=(0, 1), own=True)
+
+    MA[...] = jnp.zeros_like(MA)
     ACC[...] = jnp.zeros_like(ACC)
+
+    def fold(q):
+        MA[...] += dot(WT[q], WO[q])
 
     def add(q):
         ACC[...] += dot(XB[q].reshape(micro * tok, blk), WI[q])
         WT[q] = WI[q].T
+        pl.when(ahead)(functools.partial(fold, q))
 
     for copy in local:
         copy.wait()
@@ -156,6 +181,14 @@
         decayed = jnp.exp(-rates[0, h] * jnp.maximum(offset, 0.0))
         TAB[h] = jnp.where(offset >= 0.0, decayed, 0.0)
 
+    @pl.when(ahead)
+    def _():
+        for h in range(2):
+            up_copy(h).wait_recv()
+
+    for h in range(2):
+        for target in (xp, xm, zp, core):
+            push(r, h, target, arrays=(2,))
     add(r)
     arrive(xm, 0)
     push(xm, 0, xp)
@@ -215,6 +248,7 @@
     arrive(other(xoz), 1)
     add(other(xoz))
 
+    MM[...] = MA[...].astype(BF)
     failed = order[ndp - 1]
     live = jnp.where(r == failed, 0.0, 1.0).astype(F32)
     mine = pl.ds(pl.multiple_of(slot * tok, tok), tok)
@@ -320,6 +354,27 @@
             device_id=(jnp.maximum(s - ny, 0), r), device_id_type=MESH,
         )
 
+    def dr_copy(m):
+        return pltpu.make_async_remote_copy(
+            src_ref=DRN.at[m], dst_ref=DRB.at[m],
+            send_sem=dsend.at[m], recv_sem=drecv.at[m],
+            device_id=(jnp.maximum(s - 1, 0), r), device_id_type=MESH,
+        )
+
+    def dr_relay(m):
+        return pltpu.make_async_remote_copy(
+            src_ref=DRN.at[m], dst_ref=RD.at[m],
+            send_sem=dsend.at[m], recv_sem=erecv.at[m],
+            device_id=(jnp.minimum(s + ny - 1, last), r), device_id_type=MESH,
+        )
+
+    def dr_pass(m):
+        return pltpu.make_async_remote_copy(
+            src_ref=RD.at[m], dst_ref=DRB.at[m],
+            send_sem=esend.at[m], recv_sem=drecv.at[m],
+            device_id=(jnp.maximum(s - ny, 0), r), device_id_type=MESH,
+        )
+
     def q_copy(m, i):
         q = peer(2 * i)
         return pltpu.make_async_remote_copy(
@@ -382,15 +437,17 @@
     inline = s < nsec // 3 + 1
 
     def step(m, carry):
-        d_mixed = jnp.zeros((tok, cols), F32)
-        for k in range(nchunk):
-            @pl.when(s < last)
-            def _():
-                chunk_copy(m, k).wait_recv()
-
-            for j in range(k * per, (k + 1) * per):
-                d_mixed += dot(DY[m, j], WO[j])
-        d_mixed = d_mixed.astype(BF)
+        @pl.when(direct)
+        def _():
+            total = jnp.zeros((tok, cols), F32)
+            for k in range(nchunk):
+                pl.when(s < last)(chunk_copy(m, k).wait_recv)
+                for j in range(k * per, (k + 1) * per):
+                    total += dot(DY[m, j], WS[j])
+            DRB[m] = total.astype(BF)
+
+        pl.when(s < last - 1)(dr_copy(m).wait_recv)
+        d_mixed = DRB[m]
         parts = [[], [], []]
         for h in range(heads):
             q = QKV[m, :, h * hd : (h + 1) * hd]
@@ -402,7 +459,26 @@
             parts[1].append(dot_tn(d_score, q).astype(BF))
             parts[2].append(dot_tn(SC[m, h], dr).astype(BF))
         d_all = jnp.concatenate(parts[0] + parts[1] + parts[2], axis=1)
+
+        @pl.when(ahead)
+        def _():
+            PA[...] = dot(d_all, MM[...])
+
         for k in range(nchunk):
+            pl.when(s < last - 1)(chunk_copy(m, k).wait_recv)
+
+            @pl.when(ahead)
+            def _():
+                total = PA[...]
+                for j in range(k * per, (k + 1) * per):
+                    total += dot(DY[m, j], WO[j])
+                if k < nchunk - 1:
+                    PA[...] = total
+                else:
+                    DRN[m] = total.astype(BF)
+                    pl.when(to_next)(dr_copy(m).start)
+                    pl.when(to_relay)(dr_relay(m).start)
+
             for j in range(k * per, (k + 1) * per):
                 back = dot(d_all, WT[j])
                 NX[m, j] = (DY[m, j].astype(F32) + back).astype(BF)
@@ -438,6 +514,9 @@
     def _():
         def forward(m, carry):
             for k in range(nchunk):
+                if k == nchunk - 1:
+                    dr_relay(m).wait_recv()
+                    dr_pass(m).start()
                 relay_copy(m, k).wait_recv()
                 pass_on(m, k).start()
             return carry
@@ -480,8 +559,10 @@
     out2 = pltpu.make_async_copy(GI, grad_in.at[0], loc.at[2])
     out2.start()
 
-    for copy in sent:
-        copy.wait_send()
+    for copy, cond in sent:
+        pl.when(cond)(copy.wait_send)
+    for h in range(2):
+        pl.when(s < last - 1)(up_copy(h).wait_send)
     for i in range(1, ndp):
         x_copy(i).wait_send()
     for i in range(1, ndp // 2):
@@ -489,6 +570,8 @@
     r_swap(plane).wait_send()
 
     def drain(m, carry):
+        pl.when(ahead)(dr_copy(m).wait_send)
+
         @pl.when(s > 0)
         def _():
             for k in range(nchunk):
@@ -496,6 +579,7 @@
 
         @pl.when(node)
         def _():
+            dr_pass(m).wait_send()
             for k in range(nchunk):
                 pass_on(m, k).wait_send()
 
@@ -539,7 +623,14 @@
         scratch_shapes=[
             pltpu.VMEM((ndp, blk, 3 * cols), BF),
             pltpu.VMEM((ndp, blk, cols), BF),
+            pltpu.VMEM((ndp, blk, cols), BF),
             pltpu.VMEM((ndp, 3 * cols, blk), BF),
+            pltpu.VMEM((3 * cols, cols), F32),
+            pltpu.VMEM((3 * cols, cols), BF),
+            pltpu.VMEM((micro, tok, cols), BF),
+            pltpu.VMEM((micro, tok, cols), BF),
+            pltpu.VMEM((micro, tok, cols), BF),
+            pltpu.VMEM((tok, cols), F32),
             pltpu.VMEM((ndp, micro, tok, blk), BF),
             pltpu.VMEM((micro, ndp, tok, blk), BF),
             pltpu.VMEM((micro, ndp, tok, blk), BF),
@@ -554,13 +645,17 @@
             pltpu.VMEM((micro, ndp * tok, cols), BF),
             pltpu.VMEM((blk, 3 * cols), F32),
             pltpu.VMEM((blk, cols), F32),
-            dma((2 + ndp,)),
-            dma((64,)),
-            dma((ndp, 2, 2)),
+            dma((4 + ndp,)),
+            dma((96,)),
+            dma((ndp, 2, 3)),
             dma((micro, nchunk)),
             dma((micro, nchunk)),
             dma((micro, nchunk)),
             dma((micro, nchunk)),
+            dma((micro,)),
+            dma((micro,)),
+            dma((micro,)),
+            dma((micro,)),
             dma((ndp,)),
             dma((ndp,)),
             dma((ndp // 2,)),

time: 251 us -> 252 us (level)
  Pallas kernels: 243 us -> 246 us
where the time goes in v5:
time: 252 us; the launch traced here: 251 us
  Pallas kernels  246 us (98%)
  local copies, waits for them, and re-layouts  4.36 us (2%)
    pallas_call x1, Pallas kernels, shards(): pl.pallas_call(functools.partial(kernel, dims), name='retention_stack_bac...  246 us

profile of v5, /device:TPU:33, one launch (start us, length us, event | category | flops | bytes accessed | tf_op | source)
XLA Modules:
  0.0 250.7 jit_solution(1722552543273527504)
XLA Ops:
  0.6 245.6 %retention_stack_back.1 = (bf16[1,4,32,4096]{3,2,1,0:T(8,128)(2,1)}, f32[1,256,1152]{2,1,0:T(8,128)}, f32[1,256,384]{2,1,0:T(8,128)}) custom-call(bf16[1,4,32,4096]{3,2,1,0:T(8,128)(2,1)} %acts.1, bf16[4,32,4096]{2,1,0:T(8,128)(2,1)} %out_grad.1, bf16[1,256,1152]{2,1,0:T(8,128)(2,1)} %w_in.1, bf16[1,256,384]{2,1,0:T(8,128)(2,1)} %w_out.1, f32[1,3]{1,0:T(1,128)} %rates.1, ...), custom_call_target="tpu_custom_call" | custom-call | flops 6000000000 | bytes 8000000 | tf_op jit(solution)/shard_map/retention_stack_back/pallas_call | solution.py:613
  246.3 0.0 copy-start
  246.3 2.4 copy.12
  248.7 0.0 copy-done
  248.7 0.0 copy-start.1
  248.7 1.0 copy.13
  249.7 0.2 copy-done.1
  249.9 0.7 copy.14
Async XLA Ops:
  246.3 2.4 copy-start
  248.7 1.2 copy-start.1

commit v6 on v5

--- a/solution.py
+++ b/solution.py
@@ -28,7 +28,7 @@
     dims,
     acts, out_grad, w_in, w_out, rates, order,
     in_grad, grad_in, grad_out,
-    WI, WS, WO, WT, MA, MM, DRB, DRN, RD, PA, XB, DY, NX, RB, ACC, QKV, SC, TAB, XS, DS, DQ, RA, GI, GO,
+    WI, WS, WO, WT, MA, MM, DRB, DRN, RD, XB, DY, NX, RB, ACC, QKV, SC, TAB, XS, DS, DQ, RA, GI, GO,
     loc, wsend, wrecv, csend, crecv, bsend, brecv, dsend, drecv, esend, erecv, xsend, xrecv, rsend, rrecv, qsend, qrecv, ysend, yrecv, outsem,
 ):
     nsec, ndp, micro, tok, width, heads, hd, nchunk = dims
@@ -44,8 +44,9 @@
     lead = min(4, nsec // 4)
     ny = 4 if nsec >= 16 else 2
     y = lax.rem(s, ny)
-    direct = s >= last - 1
-    ahead = (s > 0) & (s < last)
+    first = last - 2
+    direct = s >= first
+    ahead = (s > 0) & (s <= first)
     to_relay = (s > 0) & (y == 0) & (zl == 0)
     to_next = (s > 0) & ((y != 0) | (zl != 0))
     node = (s >= ny) & (y == ny - 1) & (zl == 0)
@@ -98,7 +99,7 @@
         jnp.where(to_next, 1, 0)
         + jnp.where(to_relay, 1, 0)
         + jnp.where(node, 1, 0)
-        + jnp.where(s < last - 1, 1, 0)
+        + jnp.where(s < first, 1, 0)
     )
     pl.semaphore_wait(barrier, ndp - 1 + receivers)
 
@@ -148,7 +149,7 @@
         )
 
     for h in range(2):
-        pl.when(s < last - 1)(up_copy(h).start)
+        pl.when(s < first)(up_copy(h).start)
     for h in range(2):
         for target in (xp, xm, zp, core):
             push(r, h, target, arrays=(0, 1), own=True)
@@ -398,21 +399,31 @@
             device_id=(s, core), device_id_type=MESH,
         )
 
+    def both(q):
+        return pl.ds(2 * (q // 2), 2)
+
     def y_copy(m, i):
-        q = peer(i)
-        return pltpu.make_async_remote_copy(
-            src_ref=DY.at[m, q], dst_ref=DS.at[m, mine],
+        q = peer(2 * i)
+        return pltpu.make_async_remote_copy(
+            src_ref=DY.at[m, both(q)], dst_ref=DS.at[m, :, mine],
             send_sem=ysend.at[m, i], recv_sem=yrecv.at[m, i],
             device_id=(s, q), device_id_type=MESH,
         )
 
     def y_wait(m, i):
-        q = lax.rem(r - i + ndp, ndp)
+        q = lax.rem(r - 2 * i + ndp, ndp)
         pltpu.make_async_remote_copy(
-            src_ref=DY.at[m, q], dst_ref=DS.at[m, rows_of(q)],
+            src_ref=DY.at[m, both(q)], dst_ref=DS.at[m, :, rows_of(q)],
             send_sem=ysend.at[m, i], recv_sem=yrecv.at[m, i],
             device_id=(s, q), device_id_type=MESH,
         ).wait_recv()
+
+    def y_swap(m, which, rows):
+        return pltpu.make_async_remote_copy(
+            src_ref=DS.at[m, which, rows], dst_ref=DS.at[m, which, rows],
+            send_sem=ysend.at[m, 0], recv_sem=yrecv.at[m, 0],
+            device_id=(s, core), device_id_type=MESH,
+        )
 
     @pl.when(s == last)
     def _():
@@ -423,30 +434,27 @@
 
     def settle(m):
         q_swap(m, foreign).wait_recv()
-        for i in range(1, ndp):
-            y_wait(m, i)
+        y_swap(m, c, foreign).wait_recv()
         GI[...] += dot_tn(XS[m], DQ[m])
-        GO[...] += dot_tn(DS[m], RA[m])
+        GO[...] += dot_tn(DS[m, c], RA[m])
 
     def exchange(m):
         for i in range(1, ndp // 2):
             q_copy(m, i).start()
-        for i in range(1, ndp):
+        for i in range(1, ndp // 2):
             y_copy(m, i).start()
 
-    inline = s < nsec // 3 + 1
+    inline = s < nsec // 4
 
     def step(m, carry):
         @pl.when(direct)
         def _():
-            total = jnp.zeros((tok, cols), F32)
             for k in range(nchunk):
                 pl.when(s < last)(chunk_copy(m, k).wait_recv)
-                for j in range(k * per, (k + 1) * per):
-                    total += dot(DY[m, j], WS[j])
-            DRB[m] = total.astype(BF)
-
-        pl.when(s < last - 1)(dr_copy(m).wait_recv)
+            rows = jnp.concatenate([DY[m, j] for j in range(ndp)], axis=1)
+            DRB[m] = dot(rows, WS[...].reshape(width, cols)).astype(BF)
+
+        pl.when(s < first)(dr_copy(m).wait_recv)
         d_mixed = DRB[m]
         parts = [[], [], []]
         for h in range(heads):
@@ -460,26 +468,17 @@
             parts[2].append(dot_tn(SC[m, h], dr).astype(BF))
         d_all = jnp.concatenate(parts[0] + parts[1] + parts[2], axis=1)
 
-        @pl.when(ahead)
-        def _():
-            PA[...] = dot(d_all, MM[...])
-
+        total = dot(d_all, MM[...])
         for k in range(nchunk):
-            pl.when(s < last - 1)(chunk_copy(m, k).wait_recv)
-
-            @pl.when(ahead)
-            def _():
-                total = PA[...]
-                for j in range(k * per, (k + 1) * per):
-                    total += dot(DY[m, j], WO[j])
-                if k < nchunk - 1:
-                    PA[...] = total
-                else:
-                    DRN[m] = total.astype(BF)
-                    pl.when(to_next)(dr_copy(m).start)
-                    pl.when(to_relay)(dr_relay(m).start)
-
-            for j in range(k * per, (k + 1) * per):
+            pl.when(s < first)(chunk_copy(m, k).wait_recv)
+            span = range(k * per, (k + 1) * per)
+            rows = jnp.concatenate([DY[m, j] for j in span], axis=1)
+            total += dot(rows, WO[k * per : (k + 1) * per].reshape(per * blk, cols))
+            if k == nchunk - 1:
+                DRN[m] = total.astype(BF)
+                pl.when(ahead & to_next)(dr_copy(m).start)
+                pl.when(ahead & to_relay)(dr_relay(m).start)
+            for j in span:
                 back = dot(d_all, WT[j])
                 NX[m, j] = (DY[m, j].astype(F32) + back).astype(BF)
 
@@ -492,7 +491,7 @@
                 relay_copy(m, k).start()
 
         DQ[m, mine] = (d_all.astype(F32) * live).astype(BF)
-        DS[m, mine] = DY[m, r]
+        DS[m, :, mine] = DY[m, both(r)]
 
         @pl.when(inline)
         def _():
@@ -525,7 +524,7 @@
 
     pl.when(s >= last - lead)(exchange_early)
 
-    @pl.when(s >= nsec // 3 + 1)
+    @pl.when(s >= nsec // 4)
     def _():
         def send(m, carry):
             exchange(m)
@@ -539,6 +538,9 @@
         for i in range(1, ndp // 2):
             q_wait(m, i)
         q_swap(m, plane).start()
+        for i in range(1, ndp // 2):
+            y_wait(m, i)
+        y_swap(m, 1 - c, plane).start()
 
     swap(0)
 
@@ -549,9 +551,8 @@
 
     lax.fori_loop(0, micro - 1, finish, 0)
     m = micro - 1
-    for i in range(1, ndp):
-        y_wait(m, i)
-    GO[...] = (GO[...] + dot_tn(DS[m], RA[m])) * scale
+    y_swap(m, c, foreign).wait_recv()
+    GO[...] = (GO[...] + dot_tn(DS[m, c], RA[m])) * scale
     out1 = pltpu.make_async_copy(GO, grad_out.at[0], loc.at[1])
     out1.start()
     q_swap(m, foreign).wait_recv()
@@ -562,7 +563,7 @@
     for copy, cond in sent:
         pl.when(cond)(copy.wait_send)
     for h in range(2):
-        pl.when(s < last - 1)(up_copy(h).wait_send)
+        pl.when(s < first)(up_copy(h).wait_send)
     for i in range(1, ndp):
         x_copy(i).wait_send()
     for i in range(1, ndp // 2):
@@ -586,8 +587,9 @@
         for i in range(1, ndp // 2):
             q_copy(m, i).wait_send()
         q_swap(m, plane).wait_send()
-        for i in range(1, ndp):
+        for i in range(1, ndp // 2):
             y_copy(m, i).wait_send()
+        y_swap(m, 1 - c, plane).wait_send()
         return carry
 
     lax.fori_loop(0, micro, drain, 0)
@@ -605,7 +607,7 @@
     heads = decay_rate.shape[1]
     hd = cols // heads
     blk = width // ndp
-    nchunk = 4
+    nchunk = 2
     dims = (nsec, ndp, micro, tok, width, heads, hd, nchunk)
     dma = pltpu.SemaphoreType.DMA
     any_spec = pl.BlockSpec(memory_space=pl.ANY)
@@ -630,7 +632,6 @@
             pltpu.VMEM((micro, tok, cols), BF),
             pltpu.VMEM((micro, tok, cols), BF),
             pltpu.VMEM((micro, tok, cols), BF),
-            pltpu.VMEM((tok, cols), F32),
             pltpu.VMEM((ndp, micro, tok, blk), BF),
             pltpu.VMEM((micro, ndp, tok, blk), BF),
             pltpu.VMEM((micro, ndp, tok, blk), BF),
@@ -640,7 +641,7 @@
             pltpu.VMEM((micro, heads, tok, tok), BF),
             pltpu.VMEM((heads, tok, tok), F32),
             pltpu.VMEM((micro, ndp * tok, blk), BF),
-            pltpu.VMEM((micro, ndp * tok, blk), BF),
+            pltpu.VMEM((micro, 2, ndp * tok, blk), BF),
             pltpu.VMEM((micro, ndp * tok, 3 * cols), BF),
             pltpu.VMEM((micro, ndp * tok, cols), BF),
             pltpu.VMEM((blk, 3 * cols), F32),
@@ -662,8 +663,8 @@
             dma((ndp // 2,)),
             dma((micro, ndp // 2)),
             dma((micro, ndp // 2)),
-            dma((micro, ndp)),
-            dma((micro, ndp)),
+            dma((micro, ndp // 2)),
+            dma((micro, ndp // 2)),
             dma((ndp,)),
         ],
         compiler_params=pltpu.CompilerParams(

time: 252 us -> 240 us (0.952)
  Pallas kernels: 246 us -> 235 us
    pallas_call x1, Pallas kernels: 246 us -> 235 us  [shards(): pl.pallas_call(functools.partial(kernel, dims), name='retention_stack_bac...]
where the time goes in v6:
time: 240 us
  Pallas kernels  235 us (98%)
  local copies, waits for them, and re-layouts  4.36 us (2%)
    pallas_call x1, Pallas kernels, shards(): pl.pallas_call(functools.partial(kernel, dims), name='retention_stack_bac...  235 us

profile of v6, /device:TPU:33, one launch (start us, length us, event | category | flops | bytes accessed | tf_op | source)
XLA Modules:
  0.0 240.2 jit_solution(10947310704168373438)
XLA Ops:
  0.6 235.2 %retention_stack_back.1 = (bf16[1,4,32,4096]{3,2,1,0:T(8,128)(2,1)}, f32[1,256,1152]{2,1,0:T(8,128)}, f32[1,256,384]{2,1,0:T(8,128)}) custom-call(bf16[1,4,32,4096]{3,2,1,0:T(8,128)(2,1)} %acts.1, bf16[4,32,4096]{2,1,0:T(8,128)(2,1)} %out_grad.1, bf16[1,256,1152]{2,1,0:T(8,128)(2,1)} %w_in.1, bf16[1,256,384]{2,1,0:T(8,128)(2,1)} %w_out.1, f32[1,3]{1,0:T(1,128)} %rates.1, ...), custom_call_target="tpu_custom_call" | custom-call | flops 6000000000 | bytes 8000000 | tf_op jit(solution)/shard_map/retention_stack_back/pallas_call | solution.py:615
  235.8 0.0 copy-start
  235.8 2.4 copy.12
  238.2 0.0 copy-done
  238.2 0.0 copy-start.1
  238.2 1.0 copy.13
  239.2 0.2 copy-done.1
  239.4 0.7 copy.14
Async XLA Ops:
  235.8 2.4 copy-start
  238.2 1.2 copy-start.1

commit v7 on v6

--- a/solution.py
+++ b/solution.py
@@ -180,7 +180,7 @@
     offset = (spot_t - spot_j).astype(F32)
     for h in range(heads):
         decayed = jnp.exp(-rates[0, h] * jnp.maximum(offset, 0.0))
-        TAB[h] = jnp.where(offset >= 0.0, decayed, 0.0)
+        TAB[h] = jnp.where(offset >= 0.0, decayed, 0.0) / hd
 
     @pl.when(ahead)
     def _():
@@ -249,7 +249,10 @@
     arrive(other(xoz), 1)
     add(other(xoz))
 
-    MM[...] = MA[...].astype(BF)
+    @pl.when(ahead)
+    def _():
+        MM[...] = MA[...].astype(BF)
+
     failed = order[ndp - 1]
     live = jnp.where(r == failed, 0.0, 1.0).astype(F32)
     mine = pl.ds(pl.multiple_of(slot * tok, tok), tok)
@@ -259,11 +262,7 @@
         for h in range(heads):
             q = QKV[m, :, h * hd : (h + 1) * hd]
             k = QKV[m, :, cols + h * hd : cols + (h + 1) * hd]
-            v = QKV[m, :, 2 * cols + h * hd : 2 * cols + (h + 1) * hd]
-            score = (dot_nt(q, k) * TAB[h] / hd).astype(BF)
-            SC[m, h] = score
-            mixed = dot(score, v).astype(BF)
-            RA[m, mine, h * hd : (h + 1) * hd] = (mixed.astype(F32) * live).astype(BF)
+            SC[m, h] = (dot_nt(q, k) * TAB[h]).astype(BF)
 
     plane = pl.ds(pl.multiple_of(c * (ndp // 2) * tok, tok), (ndp // 2) * tok)
     foreign = pl.ds(pl.multiple_of((1 - c) * (ndp // 2) * tok, tok), (ndp // 2) * tok)
@@ -313,6 +312,11 @@
     own_x = pltpu.make_async_copy(XB.at[r], XS.at[:, mine], loc.at[0])
 
     def exchange_early():
+        for m in range(micro):
+            for h in range(heads):
+                v = QKV[m, :, 2 * cols + h * hd : 2 * cols + (h + 1) * hd]
+                mixed = dot(SC[m, h], v).astype(BF)
+                RA[m, mine, h * hd : (h + 1) * hd] = (mixed.astype(F32) * live).astype(BF)
         for i in range(1, ndp // 2):
             r_copy(i).start()
         own_x.start()
@@ -325,6 +329,15 @@
         for i in range(1, ndp):
             x_wait(i)
         r_swap(foreign).wait_recv()
+        for i in range(1, ndp):
+            x_copy(i).wait_send()
+        for i in range(1, ndp // 2):
+            r_copy(i).wait_send()
+        r_swap(plane).wait_send()
+        for copy, cond in sent:
+            pl.when(cond)(copy.wait_send)
+        for h in range(2):
+            pl.when(s < first)(up_copy(h).wait_send)
 
     GI[...] = jnp.zeros_like(GI)
     GO[...] = jnp.zeros_like(GO)
@@ -438,11 +451,17 @@
         GI[...] += dot_tn(XS[m], DQ[m])
         GO[...] += dot_tn(DS[m, c], RA[m])
 
+    def exchange_q(m):
+        for i in range(1, ndp // 2):
+            q_copy(m, i).start()
+
+    def exchange_y(m):
+        for i in range(1, ndp // 2):
+            y_copy(m, i).start()
+
     def exchange(m):
-        for i in range(1, ndp // 2):
-            q_copy(m, i).start()
-        for i in range(1, ndp // 2):
-            y_copy(m, i).start()
+        exchange_q(m)
+        exchange_y(m)
 
     inline = s < nsec // 4
 
@@ -462,15 +481,19 @@
             k = QKV[m, :, cols + h * hd : cols + (h + 1) * hd]
             v = QKV[m, :, 2 * cols + h * hd : 2 * cols + (h + 1) * hd]
             dr = d_mixed[:, h * hd : (h + 1) * hd]
-            d_score = (dot_nt(dr, v) * TAB[h] / hd).astype(BF)
+            d_score = (dot_nt(dr, v) * TAB[h]).astype(BF)
             parts[0].append(dot(d_score, k).astype(BF))
             parts[1].append(dot_tn(d_score, q).astype(BF))
             parts[2].append(dot_tn(SC[m, h], dr).astype(BF))
         d_all = jnp.concatenate(parts[0] + parts[1] + parts[2], axis=1)
 
+        DQ[m, mine] = (d_all.astype(F32) * live).astype(BF)
+        pl.when(s == 0)(functools.partial(exchange_q, m))
         total = dot(d_all, MM[...])
         for k in range(nchunk):
             pl.when(s < first)(chunk_copy(m, k).wait_recv)
+            if k == nchunk - 1:
+                pl.when(s == 0)(functools.partial(exchange_y, m))
             span = range(k * per, (k + 1) * per)
             rows = jnp.concatenate([DY[m, j] for j in span], axis=1)
             total += dot(rows, WO[k * per : (k + 1) * per].reshape(per * blk, cols))
@@ -490,10 +513,9 @@
             def _():
                 relay_copy(m, k).start()
 
-        DQ[m, mine] = (d_all.astype(F32) * live).astype(BF)
         DS[m, :, mine] = DY[m, both(r)]
 
-        @pl.when(inline)
+        @pl.when(inline & (s > 0))
         def _():
             exchange(m)
 
@@ -559,16 +581,6 @@
     GI[...] = (GI[...] + dot_tn(XS[m], DQ[m])) * scale
     out2 = pltpu.make_async_copy(GI, grad_in.at[0], loc.at[2])
     out2.start()
-
-    for copy, cond in sent:
-        pl.when(cond)(copy.wait_send)
-    for h in range(2):
-        pl.when(s < first)(up_copy(h).wait_send)
-    for i in range(1, ndp):
-        x_copy(i).wait_send()
-    for i in range(1, ndp // 2):
-        r_copy(i).wait_send()
-    r_swap(plane).wait_send()
 
     def drain(m, carry):
         pl.when(ahead)(dr_copy(m).wait_send)

time: 240 us -> 235 us (0.979)
  Pallas kernels: 235 us -> 230 us
    pallas_call x1, Pallas kernels: 235 us -> 230 us  [shards(): pl.pallas_call(functools.partial(kernel, dims), name='retention_stack_bac...]
where the time goes in v7:
time: 235 us
  Pallas kernels  230 us (98%)
  local copies, waits for them, and re-layouts  4.36 us (2%)
    pallas_call x1, Pallas kernels, shards(): pl.pallas_call(functools.partial(kernel, dims), name='retention_stack_bac...  230 us

profile of v7, /device:TPU:33, one launch (start us, length us, event | category | flops | bytes accessed | tf_op | source)
XLA Modules:
  0.0 234.6 jit_solution(7809261130422194502)
XLA Ops:
  0.6 229.6 %retention_stack_back.1 = (bf16[1,4,32,4096]{3,2,1,0:T(8,128)(2,1)}, f32[1,256,1152]{2,1,0:T(8,128)}, f32[1,256,384]{2,1,0:T(8,128)}) custom-call(bf16[1,4,32,4096]{3,2,1,0:T(8,128)(2,1)} %acts.1, bf16[4,32,4096]{2,1,0:T(8,128)(2,1)} %out_grad.1, bf16[1,256,1152]{2,1,0:T(8,128)(2,1)} %w_in.1, bf16[1,256,384]{2,1,0:T(8,128)(2,1)} %w_out.1, f32[1,3]{1,0:T(1,128)} %rates.1, ...), custom_call_target="tpu_custom_call" | custom-call | flops 6000000000 | bytes 8000000 | tf_op jit(solution)/shard_map/retention_stack_back/pallas_call | solution.py:627
  230.2 0.0 copy-start
  230.2 2.4 %copy.12 = bf16[1,4,32,4096]{3,2,1,0:T(8,128)(2,1)} copy(bf16[1,4,32,4096]{3,2,1,0:T(8,128)(2,1)} %get-tuple-element.6) | data formatting | bytes 2097152
  232.6 0.0 copy-done
  232.6 0.0 copy-start.1
  232.6 1.0 copy.13
  233.6 0.2 copy-done.1
  233.8 0.7 copy.14
Async XLA Ops:
  230.2 2.4 %copy-start = (f32[1,256,1152]{2,1,0:T(8,128)S(1)}, f32[1,256,1152]{2,1,0:T(8,128)}, u32[]{:S(2)}) copy-start(f32[1,256,1152]{2,1,0:T(8,128)} %get-tuple-element.7) | copy-start | bytes 3538948
  232.6 1.2 copy-start.1

commit v8 on v7

--- a/solution.py
+++ b/solution.py
@@ -463,7 +463,7 @@
         exchange_q(m)
         exchange_y(m)
 
-    inline = s < nsec // 4
+    inline = s < max(1, nsec // 5)
 
     def step(m, carry):
         @pl.when(direct)
@@ -546,7 +546,7 @@
 
     pl.when(s >= last - lead)(exchange_early)
 
-    @pl.when(s >= nsec // 4)
+    @pl.when(s >= max(1, nsec // 5))
     def _():
         def send(m, carry):
             exchange(m)
@@ -564,11 +564,33 @@
             y_wait(m, i)
         y_swap(m, 1 - c, plane).start()
 
+    def drain(m):
+        pl.when(ahead)(dr_copy(m).wait_send)
+
+        @pl.when(s > 0)
+        def _():
+            for k in range(nchunk):
+                chunk_copy(m, k).wait_send()
+
+        @pl.when(node)
+        def _():
+            dr_pass(m).wait_send()
+            for k in range(nchunk):
+                pass_on(m, k).wait_send()
+
+        for i in range(1, ndp // 2):
+            q_copy(m, i).wait_send()
+        q_swap(m, plane).wait_send()
+        for i in range(1, ndp // 2):
+            y_copy(m, i).wait_send()
+        y_swap(m, 1 - c, plane).wait_send()
+
     swap(0)
 
     def finish(m, carry):
         swap(m + 1)
         settle(m)
+        drain(m)
         return carry
 
     lax.fori_loop(0, micro - 1, finish, 0)
@@ -582,29 +604,7 @@
     out2 = pltpu.make_async_copy(GI, grad_in.at[0], loc.at[2])
     out2.start()
 
-    def drain(m, carry):
-        pl.when(ahead)(dr_copy(m).wait_send)
-
-        @pl.when(s > 0)
-        def _():
-            for k in range(nchunk):
-                chunk_copy(m, k).wait_send()
-
-        @pl.when(node)
-        def _():
-            dr_pass(m).wait_send()
-            for k in range(nchunk):
-                pass_on(m, k).wait_send()
-
-        for i in range(1, ndp // 2):
-            q_copy(m, i).wait_send()
-        q_swap(m, plane).wait_send()
-        for i in range(1, ndp // 2):
-            y_copy(m, i).wait_send()
-        y_swap(m, 1 - c, plane).wait_send()
-        return carry
-
-    lax.fori_loop(0, micro, drain, 0)
+    drain(micro - 1)
     for copy in writes:
         copy.wait()
     out1.wait()

time: 235 us -> 236 us (level)
  no operation moved by 1% of the time
where the time goes in v8:
time: 236 us; the launch traced here: 235 us
  Pallas kernels  230 us (97%)
  local copies, waits for them, and re-layouts  4.36 us (2%)
    pallas_call x1, Pallas kernels, shards(): pl.pallas_call(functools.partial(kernel, dims), name='retention_stack_bac...  230 us

profile of v8, /device:TPU:33, one launch (start us, length us, event | category | flops | bytes accessed | tf_op | source)
XLA Modules:
  0.0 234.6 jit_solution(13103752119045967663)
XLA Ops:
  0.6 229.5 %retention_stack_back.1 = (bf16[1,4,32,4096]{3,2,1,0:T(8,128)(2,1)}, f32[1,256,1152]{2,1,0:T(8,128)}, f32[1,256,384]{2,1,0:T(8,128)}) custom-call(bf16[1,4,32,4096]{3,2,1,0:T(8,128)(2,1)} %acts.1, bf16[4,32,4096]{2,1,0:T(8,128)(2,1)} %out_grad.1, bf16[1,256,1152]{2,1,0:T(8,128)(2,1)} %w_in.1, bf16[1,256,384]{2,1,0:T(8,128)(2,1)} %w_out.1, f32[1,3]{1,0:T(1,128)} %rates.1, ...), custom_call_target="tpu_custom_call" | custom-call | flops 6000000000 | bytes 8000000 | tf_op jit(solution)/shard_map/retention_stack_back/pallas_call | solution.py:627
  230.2 0.0 copy-start
  230.2 2.4 %copy.12 = bf16[1,4,32,4096]{3,2,1,0:T(8,128)(2,1)} copy(bf16[1,4,32,4096]{3,2,1,0:T(8,128)(2,1)} %get-tuple-element.6) | data formatting | bytes 2097152
  232.6 0.0 copy-done
  232.6 0.0 copy-start.1
  232.6 1.0 copy.13
  233.6 0.2 copy-done.1
  233.8 0.7 copy.14
Async XLA Ops:
  230.2 2.4 %copy-start = (f32[1,256,1152]{2,1,0:T(8,128)S(1)}, f32[1,256,1152]{2,1,0:T(8,128)}, u32[]{:S(2)}) copy-start(f32[1,256,1152]{2,1,0:T(8,128)} %get-tuple-element.7) | copy-start | bytes 3538948
  232.6 1.2 copy-start.1
